TPU v7x, 256 devices: a whole 4x4x8 slice. The times are simulated.
256 devices in a mesh: row: 16 (over y, x_lo, core), col: 16 (over z, x_hi).
Axes of the slice: x: 4 (x_hi: 2, x_lo: 2; x = x_hi * 2 + x_lo), y: 4, z: 8, core: 2. Of those that a mesh axis runs over, the one named last changes fastest.
Arguments:
- inverse_rows: float32 [16384, 16384], P('col', 'row'), may hold values from -0.5 to 0.5
- panels: float32 [16, 16384, 256], P('col', 'row'), may hold values from -0.75 to 0.75
- diag_inverse: float32 [2, 256, 256], replicated, may hold values from -12 to 12
- pattern: int32 [2, 64], replicated, may hold values 0 or 1
- owner_slot: int32 [2], replicated, may hold values from 0 to 15, as said below
Outputs:
- inverse_column: float32 [2, 16384, 256], P(None, 'row')
- inverse_row: float32 [2, 256, 16384], P(None, None, 'col')
- diag_block: float32 [2, 256, 256], replicated
Inputs may be any that keep to these rules, and one draw needn't show every extreme that they name: `owner_slot`: the two supernodes' panels lie in two different slots, one of them the last slot.
All inputs are finite; a program needn't handle non-finite values.
Results may differ from a plain program's by a relative error of at most 0.0001.
Values sent between devices are 32-bit elements; how exact they have to be, the bound alone decides.
No kernel may reach another device: no remote copies, remote signals or barrier semaphores. Data moves between devices by JAX's collectives and lax.ppermute only.
A program may use at most 64 MiB of HBM per device.

v0:
```python
import functools

import jax
import jax.numpy as jnp
import numpy as np
from jax import lax
from jax.experimental import pallas as pl
from jax.experimental.pallas import tpu as pltpu
from jax.sharding import Mesh
from jax.sharding import PartitionSpec as P

ROW = ("y", "xl", "core")
CHIP = ("y", "xl")
COL = ("z", "xh")
ALL = ROW + COL
SMEM = pl.BlockSpec(memory_space=pltpu.SMEM)
VMEM = pl.BlockSpec(memory_space=pltpu.VMEM)
ANY = pl.BlockSpec(memory_space=pl.ANY)
SWAP = [(0, 1), (1, 0)]
TRANSPOSE = [(r * 16 + c, c * 16 + r) for r in range(16) for c in range(16)]
UP = [(i, (i + 1) % 8) for i in range(8)]
DOWN = [(i, (i - 1) % 8) for i in range(8)]


def call(kernel, outs, ins, outputs, flops=0, nbytes=1 << 21, scratch=(), mib=24, **rest):
    shapes = [jax.ShapeDtypeStruct(shape, dtype) for shape, dtype in outs]
    return pl.pallas_call(
        kernel,
        out_shape=shapes if len(shapes) > 1 else shapes[0],
        in_specs=ins,
        out_specs=outputs if len(shapes) > 1 else outputs[0],
        scratch_shapes=list(scratch),
        compiler_params=pltpu.CompilerParams(vmem_limit_bytes=mib << 20),
        cost_estimate=pl.CostEstimate(flops=flops, bytes_accessed=nbytes, transcendentals=0),
        **rest,
    )


def halves(value):
    high = value.astype(jnp.bfloat16)
    low = (value - high.astype(jnp.float32)).astype(jnp.bfloat16)
    return high, low


def dot3(left, right):
    dot = functools.partial(jnp.dot, preferred_element_type=jnp.float32)
    return dot(left[0], right[1]) + dot(left[1], right[0]) + dot(left[0], right[0])


def first_kernel(number, left, right, out, high, low, right_high, right_low):
    columns = pl.ds(pl.multiple_of(number[0] * 256, 256), 256)

    @pl.when(pl.program_id(0) == 0)
    def _():
        right_high[...], right_low[...] = halves(right[:, columns])

    pair = halves(left[...])
    high[...], low[...] = pair
    out[...] = dot3(pair, (right_high[...], right_low[...]))


def second_kernel(number, high, low, right, out, right_high, right_low):
    columns = pl.ds(pl.multiple_of(number[0] * 256, 256), 256)

    @pl.when(pl.program_id(0) == 0)
    def _():
        right_high[...], right_low[...] = halves(right[:, columns])

    out[...] = dot3((high[...], low[...]), (right_high[...], right_low[...]))


def product(number, left, right):
    block = pl.BlockSpec((256, 1024), lambda i: (i, 0))
    out_block = pl.BlockSpec((256, 256), lambda i: (i, 0))
    whole = pl.BlockSpec((1024, 512), lambda i: (0, 0))
    half = pltpu.VMEM((1024, 256), jnp.bfloat16)
    kept = ((1024, 1024), jnp.bfloat16)
    out = ((1024, 256), jnp.float32)
    rest = dict(flops=3 << 29, nbytes=7 << 20, scratch=[half, half], grid=(4,))
    if len(left) == 1:
        outs, specs = [out, kept, kept], [out_block, block, block]
        return call(first_kernel, outs, [SMEM, block, whole], specs, **rest)(number, *left, right)
    return call(second_kernel, [out], [SMEM, block, block, whole], [out_block], **rest)(number, *left, right)


def chunk_kernel(slots, at, pattern, dealt, out):
    for number in range(2):
        mask = pattern[number, at[0]].astype(jnp.float32)
        out[:, number * 256 : number * 256 + 256] = mask * dealt[slots[number]]


def reduce_kernel(at, pattern, terms, column, turned):
    total = terms[0]
    for k in range(1, 8):
        total += terms[k]
    total = -(pattern[at[0], at[1]].astype(jnp.float32) * total)
    column[...] = total
    turned[...] = total.T


def inner_kernel(at, left, right, out):
    rows = pl.ds(pl.multiple_of(at[0] * 128, 128), 128)
    columns = pl.ds(pl.multiple_of(at[1] * 256, 256), 256)
    inner = dot3(halves(left[rows, columns].T), halves(right[...]))
    for k in range(16):
        out[k] = inner[k * 16 : k * 16 + 16]


def rows_kernel(core, mine, other, out):
    for k in range(8):
        columns = slice(k * 128, k * 128 + 128)
        out[core[0], :, columns] = mine[k]
        out[1 - core[0], :, columns] = other[k]


def diag_kernel(given, pieces, out):
    for number in range(2):
        for k in range(16):
            rows = slice(k * 16, k * 16 + 16)
            out[number, rows] = given[number, rows] - pieces[2 * k + number]


def place_kernel(z, *refs):
    *pieces, top, bottom, _, out = refs
    for number in range(2):
        for piece, index in zip(pieces, (0, 7, 6, 5, 1, 2, 3)):
            start = pl.multiple_of(lax.rem(z[0] + index, 8) * 128, 128)
            out[number, pl.ds(start, 128)] = piece[number]
        start = pl.multiple_of(lax.rem(z[0] + 4, 8) * 128, 128)
        out[number, pl.ds(start, 64)] = top[number]
        out[number, pl.ds(start + 64, 64)] = bottom[number]


def both(mine, other, first):
    return jnp.where(first, jnp.stack([mine, other]), jnp.stack([other, mine]))


def ring(block):
    half = block.shape[-2] // 2
    ups, downs = [block], [block]
    for _ in range(3):
        ups.append(lax.ppermute(ups[-1], "z", UP))
        downs.append(lax.ppermute(downs[-1], "z", DOWN))
    top = lax.ppermute(ups[-1][..., :half, :], "z", UP)
    bottom = lax.ppermute(downs[-1][..., half:, :], "z", DOWN)
    return [block] + ups[1:] + downs[1:] + [top, bottom]


def gather_rows(pieces, z):
    out = jnp.zeros((1024, pieces[0].shape[1]), jnp.float32)
    index = [z, z + 7, z + 6, z + 5, z + 1, z + 2, z + 3, z + 4, z + 4]
    for k, piece in enumerate(pieces):
        out = lax.dynamic_update_slice(out, piece, (index[k] % 8 * 128 + (64 if k == 8 else 0), 0))
    return out


def shards(inverse_rows, panels, diag_inverse, pattern, owner_slot):
    row = lax.axis_index(ROW)
    col = lax.axis_index(COL)
    chip = lax.axis_index(CHIP)
    core = lax.axis_index("core")
    z = lax.axis_index("z")
    xh = lax.axis_index("xh")

    dealt = lax.all_to_all(panels[0].reshape(16, 64, 256), COL, 0, 0, tiled=True)
    out = ((64, 512), jnp.float32)
    chunk = call(chunk_kernel, [out], [SMEM] * 3 + [VMEM], [VMEM], nbytes=1 << 18)(
        owner_slot, (row * 4 + col // 4)[None], pattern, dealt
    )
    block = both(chunk, lax.ppermute(chunk, "xh", SWAP), xh == 0).reshape(128, 512)
    masked = gather_rows(ring(block), z)

    sent, *kept = product((1 - core)[None], [inverse_rows], masked)
    received = lax.ppermute(sent, "core", SWAP)
    term = product(core[None], kept, masked) + received
    terms = lax.all_to_all(term.reshape(8, 128, 256), CHIP, 0, 0, tiled=True)
    outs = [((128, 256), jnp.float32), ((256, 128), jnp.float32)]
    at = jnp.stack([core, col * 4 + chip // 2])
    column, turned = call(reduce_kernel, outs, [SMEM, SMEM, VMEM], [VMEM, VMEM])(at, pattern, terms)

    mine = lax.ppermute(column, ALL, TRANSPOSE)
    pieces = ring(both(mine, lax.ppermute(mine, "xh", SWAP), xh == 0))

    out = ((16, 16, 256), jnp.float32)
    at = jnp.stack([z, xh])
    inner = call(inner_kernel, [out], [SMEM, VMEM, VMEM], [VMEM], flops=3 << 24)(at, masked, mine)
    inner = jnp.sum(lax.all_to_all(inner, ROW, 0, 0, tiled=True), axis=0)
    inner = lax.all_to_all(jnp.broadcast_to(inner[None], (8, 16, 256)), "z", 0, 0, tiled=True)
    inner = jnp.sum(inner, axis=0)
    inner = jnp.broadcast_to(inner[None], (32, 16, 256))
    inner = lax.all_to_all(inner, ROW + ("xh",), 0, 0, tiled=True)
    out = ((2, 256, 256), jnp.float32)
    diag = call(diag_kernel, [out], [VMEM, VMEM], [VMEM], nbytes=3 << 19)(diag_inverse, inner)

    turned = jnp.broadcast_to(turned[None], (8, 256, 128))
    turned = lax.all_to_all(turned, CHIP, 0, 0, tiled=True)
    other = lax.ppermute(turned, "core", SWAP)
    out = ((2, 256, 1024), jnp.float32)
    rows = call(rows_kernel, [out], [SMEM, VMEM, VMEM], [VMEM], nbytes=1 << 22)(core[None], turned, other)

    out = ((2, 1024, 256), jnp.float32)
    lower = call(place_kernel, [out], [SMEM] + [VMEM] * 9 + [ANY], [VMEM], nbytes=1 << 22)(
        z[None], *pieces, rows
    )
    return lower, rows, diag


def solution(mesh):
    fine = Mesh(np.asarray(mesh.devices).reshape(4, 2, 2, 8, 2), ALL)
    in_specs = (P(COL, ROW), P(COL, ROW, None), P(), P(), P())
    out_specs = (P(None, ROW, None), P(None, None, COL), P())
    return jax.shard_map(shards, mesh=fine, in_specs=in_specs, out_specs=out_specs, check_vma=False)
```

profile of v0, /device:TPU:2, one launch (start us, length us, event | category | flops | bytes accessed | tf_op | source)
XLA Modules:
  0.0 196.3 jit_solution(2984164387692581953)
XLA Ops:
  0.7 10.3 %all-to-all-start = ((f32[16,64,256]{2,1,0:T(8,128)}), f32[16,64,256]{2,1,0:T(8,128)S(1)}, u32[]{:S(2)}, u32[]{:S(2)}) async-start(f32[16,64,256]{2,1,0:T(8,128)} %bitcast.19), calls=%async_computation | async-start | bytes 2097152 | tf_op jit(solution)/shard_map/all_to_all | solution.py:165
  11.0 30.2 %all-to-all-done.dealt = f32[16,64,256]{2,1,0:T(8,128)S(1)} async-done(((f32[16,64,256]{2,1,0:T(8,128)}), f32[16,64,256]{2,1,0:T(8,128)S(1)}, u32[]{:S(2)}, u32[]{:S(2)}) %all-to-all-start) | async-done | bytes 1048608 | tf_op jit(solution)/shard_map/all_to_all | solution.py:165
  41.1 0.6 shard_map.76
  41.7 0.5 collective-permute-start
  42.2 6.0 %collective-permute-done = f32[64,512]{1,0:T(8,128)S(1)} collective-permute-done((f32[64,512]{1,0:T(8,128)S(1)}, f32[64,512]{1,0:T(8,128)S(1)}, u32[]{:S(2)}, u32[]{:S(2)}) %collective-permute-start) | collective-permute-done | bytes 131104 | tf_op jit(solution)/shard_map/ppermute | solution.py:170
  48.4 2.0 %collective-permute-start.1 = (f32[128,512]{1,0:T(8,128)S(1)}, f32[128,512]{1,0:T(8,128)S(1)}, u32[]{:S(2)}, u32[]{:S(2)}) collective-permute-start(f32[128,512]{1,0:T(8,128)S(1)} %bitcast.17), channel_id=1, source_target_pairs={{0,2},{2,4},{4,6},{6,8},{8,10},{10,12},{12,14},{14,0},{1,3},{3,5},... | collective-permute-start | bytes 786440 | tf_op jit(solution)/shard_map/ppermute | solution.py:142
  50.4 6.9 %collective-permute-done.4 = f32[128,512]{1,0:T(8,128)S(1)} collective-permute-done((f32[128,512]{1,0:T(8,128)S(1)}, f32[128,512]{1,0:T(8,128)S(1)}, u32[]{:S(2)}, u32[]{:S(2)}) %collective-permute-start.4) | collective-permute-done | bytes 262176 | tf_op jit(solution)/shard_map/ppermute | solution.py:143
  57.3 2.2 %collective-permute-start.2 = (f32[128,512]{1,0:T(8,128)S(1)}, f32[128,512]{1,0:T(8,128)S(1)}, u32[]{:S(2)}, u32[]{:S(2)}) collective-permute-start(f32[128,512]{1,0:T(8,128)S(1)} %collective-permute-done.1), channel_id=1, source_target_pairs={{0,2},{2,4},{4,6},{6,8},{8,10},{10,12},{12,14},{14,0},{1,3},{3,5},... | collective-permute-start | bytes 786440 | tf_op jit(solution)/shard_map/ppermute | solution.py:142
  59.5 6.2 %collective-permute-done.5 = f32[128,512]{1,0:T(8,128)S(1)} collective-permute-done((f32[128,512]{1,0:T(8,128)S(1)}, f32[128,512]{1,0:T(8,128)S(1)}, u32[]{:S(2)}, u32[]{:S(2)}) %collective-permute-start.5) | collective-permute-done | bytes 262176 | tf_op jit(solution)/shard_map/ppermute | solution.py:143
  65.7 1.6 collective-permute-start.6
  67.4 0.4 collective-permute-start.3
  68.2 3.9 %collective-permute-done.6 = f32[128,512]{1,0:T(8,128)S(1)} collective-permute-done((f32[128,512]{1,0:T(8,128)S(1)}, f32[128,512]{1,0:T(8,128)S(1)}, u32[]{:S(2)}, u32[]{:S(2)}) %collective-permute-start.6) | collective-permute-done | bytes 262176 | tf_op jit(solution)/shard_map/ppermute | solution.py:143
  72.1 3.6 %collective-permute-start.8 = (f32[64,512]{1,0:T(8,128)S(1)}, f32[64,512]{1,0:T(8,128)S(1)}, u32[]{:S(2)}, u32[]{:S(2)}) collective-permute-start(f32[64,512]{1,0:T(8,128)S(1)} %slice.17), channel_id=1, source_target_pairs={{0,14},{2,0},{4,2},{6,4},{8,6},{10,8},{12,10},{14,12},{1,15},{3,1}... | collective-permute-start | bytes 393224 | tf_op jit(solution)/shard_map/ppermute | solution.py:145
  75.9 6.0 %collective-permute-done.7 = f32[64,512]{1,0:T(8,128)S(1)} collective-permute-done((f32[64,512]{1,0:T(8,128)S(1)}, f32[64,512]{1,0:T(8,128)S(1)}, u32[]{:S(2)}, u32[]{:S(2)}) %collective-permute-start.7) | collective-permute-done | bytes 131104 | tf_op jit(solution)/shard_map/ppermute | solution.py:144
  82.0 2.7 %shard_map.77 = (f32[1024,256]{1,0:T(8,128)S(1)}, bf16[1024,1024]{1,0:T(8,128)(2,1)S(1)}, bf16[1024,1024]{1,0:T(8,128)(2,1)S(1)}) custom-call(s32[1]{0:T(128)} %bitcast.3.number, f32[1024,1024]{1,0:T(8,128)S(1)} %copy-done.1, f32[1024,512]{1,0:T(8,128)S(1)} %constant_dynamic-update-slice_fusion.right.left), custom_call_target="tpu_custom_call" | custom-call | flops 1610612736 | bytes 7340032 | tf_op jit(solution)/shard_map/pallas_call | solution.py:82
  84.9 2.5 %shard_map.78 = f32[1024,256]{1,0:T(8,128)S(1)} custom-call(s32[1]{0:T(128)} %bitcast.1.number.core, bf16[1024,1024]{1,0:T(8,128)(2,1)S(1)} %get-tuple-element.8.high, bf16[1024,1024]{1,0:T(8,128)(2,1)S(1)} %get-tuple-element.9.low, f32[1024,512]{1,0:T(8,128)S(1)} %constant_dynamic-update-slice_fusion.right.left), custom_call_target="tpu_custom_call" | custom-call | flops 1610612736 | bytes 7340032 | tf_op jit(solution)/shard_map/pallas_call | solution.py:83
  87.5 1.1 add.134
  88.6 6.0 %all-to-all-start.1 = ((f32[8,128,256]{2,1,0:T(8,128)}), f32[8,128,256]{2,1,0:T(8,128)S(1)}, u32[]{:S(2)}, u32[]{:S(2)}) async-start(f32[8,128,256]{2,1,0:T(8,128)} %bitcast.15), calls=%async_computation.1 | async-start | bytes 2097152 | tf_op jit(solution)/shard_map/all_to_all | solution.py:176
  94.6 15.0 %all-to-all-done.1.terms = f32[8,128,256]{2,1,0:T(8,128)S(1)} async-done(((f32[8,128,256]{2,1,0:T(8,128)}), f32[8,128,256]{2,1,0:T(8,128)S(1)}, u32[]{:S(2)}, u32[]{:S(2)}) %all-to-all-start.1) | async-done | bytes 1048608 | tf_op jit(solution)/shard_map/all_to_all | solution.py:176
  109.6 0.7 shard_map.79
  110.3 1.0 broadcast_in_dim.36
  111.3 4.7 %all-to-all-start.2 = ((f32[8,256,128]{2,1,0:T(8,128)}), f32[8,256,128]{2,1,0:T(8,128)S(1)}, u32[]{:S(2)}, u32[]{:S(2)}) async-start(f32[8,256,128]{2,1,0:T(8,128)} %broadcast_in_dim.36), calls=%async_computation.2 | async-start | bytes 2097152 | tf_op jit(solution)/shard_map/all_to_all | solution.py:196
  116.0 1.9 collective-permute-start.10
  117.9 12.4 %collective-permute-done.10.right = f32[128,256]{1,0:T(8,128)S(1)} collective-permute-done((f32[128,256]{1,0:T(8,128)S(1)}, f32[128,256]{1,0:T(8,128)S(1)}, u32[]{:S(2)}, u32[]{:S(2)}) %collective-permute-start.10) | collective-permute-done | bytes 131104 | tf_op jit(solution)/shard_map/ppermute | solution.py:181
  130.4 8.5 %all-to-all-done.2.mine = f32[8,256,128]{2,1,0:T(8,128)S(1)} async-done(((f32[8,256,128]{2,1,0:T(8,128)}), f32[8,256,128]{2,1,0:T(8,128)S(1)}, u32[]{:S(2)}, u32[]{:S(2)}) %all-to-all-start.2) | async-done | bytes 1048608 | tf_op jit(solution)/shard_map/all_to_all | solution.py:196
  138.9 1.6 shard_map.82
  140.5 6.9 %all-to-all-start.3 = ((f32[16,16,256]{2,1,0:T(8,128)}), f32[16,16,256]{2,1,0:T(8,128)S(1)}, u32[]{:S(2)}, u32[]{:S(2)}) async-start(f32[16,16,256]{2,1,0:T(8,128)} %shard_map.82), calls=%async_computation.3 | async-start | bytes 524288 | tf_op jit(solution)/shard_map/all_to_all | solution.py:187
  147.4 1.0 maximum_select_fusion.1.refs_0_
  148.4 1.8 collective-permute-start.15
  150.2 0.5 collective-permute-start.12
  150.7 3.5 %all-to-all-done.3 = f32[16,16,256]{2,1,0:T(8,128)S(1)} async-done(((f32[16,16,256]{2,1,0:T(8,128)}), f32[16,16,256]{2,1,0:T(8,128)S(1)}, u32[]{:S(2)}, u32[]{:S(2)}) %all-to-all-start.3) | async-done | bytes 262176 | tf_op jit(solution)/shard_map/all_to_all | solution.py:187
  154.2 0.7 broadcast_in_dim.37
  154.9 3.4 %all-to-all-start.4 = ((f32[8,16,256]{2,1,0:T(8,128)}), f32[8,16,256]{2,1,0:T(8,128)S(1)}, u32[]{:S(2)}, u32[]{:S(2)}) async-start(f32[8,16,256]{2,1,0:T(8,128)} %broadcast_in_dim.37), calls=%async_computation.4 | async-start | bytes 262144 | tf_op jit(solution)/shard_map/all_to_all | solution.py:188
  158.3 3.2 %collective-permute-start.16 = (f32[2,128,256]{2,1,0:T(8,128)S(1)}, f32[2,128,256]{2,1,0:T(8,128)}, u32[]{:S(2)}, u32[]{:S(2)}) collective-permute-start(f32[2,128,256]{2,1,0:T(8,128)S(1)} %collective-permute-done.15.refs_4_), channel_id=1, source_target_pairs={{0,14},{2,0},{4,2},{6,4},{8,6},{10,8},{12,10},{14,12},{1,15},{3,1}... | collective-permute-start | bytes 786440 | tf_op jit(solution)/shard_map/ppermute | solution.py:143
  161.5 6.8 %all-to-all-done.4 = f32[8,16,256]{2,1,0:T(8,128)S(1)} async-done(((f32[8,16,256]{2,1,0:T(8,128)}), f32[8,16,256]{2,1,0:T(8,128)S(1)}, u32[]{:S(2)}, u32[]{:S(2)}) %all-to-all-start.4) | async-done | bytes 131104 | tf_op jit(solution)/shard_map/all_to_all | solution.py:188
  168.3 0.9 broadcast_in_dim.38
  169.1 4.7 %all-to-all-start.5 = ((f32[32,16,256]{2,1,0:T(8,128)}), f32[32,16,256]{2,1,0:T(8,128)S(1)}, u32[]{:S(2)}, u32[]{:S(2)}) async-start(f32[32,16,256]{2,1,0:T(8,128)} %broadcast_in_dim.38), calls=%async_computation.5 | async-start | bytes 1048576 | tf_op jit(solution)/shard_map/all_to_all | solution.py:191
  173.8 0.7 collective-permute-start.17
  174.6 1.4 collective-permute-start.14
  176.0 6.5 %collective-permute-done.17.refs_6_ = f32[2,128,256]{2,1,0:T(8,128)S(1)} collective-permute-done((f32[2,128,256]{2,1,0:T(8,128)}, f32[2,128,256]{2,1,0:T(8,128)S(1)}, u32[]{:S(2)}, u32[]{:S(2)}) %collective-permute-start.17) | collective-permute-done | bytes 262176 | tf_op jit(solution)/shard_map/ppermute | solution.py:143
  182.5 0.7 slice.19
  183.2 1.8 collective-permute-start.19
  185.0 0.7 slice.18
  185.9 0.8 shard_map.83
  186.7 2.8 %shard_map.80.refs_9_ = f32[2,256,1024]{2,1,0:T(8,128)} custom-call(s32[1]{0:T(128)} %bitcast.1.number.core, f32[8,256,128]{2,1,0:T(8,128)S(1)} %all-to-all-done.2.mine, f32[8,256,128]{2,1,0:T(8,128)} %collective-permute-done.20.other), custom_call_target="tpu_custom_call" | custom-call | bytes 4194304 | tf_op jit(solution)/shard_map/pallas_call | solution.py:199
  189.5 2.6 %collective-permute-done.18.refs_7_ = f32[2,64,256]{2,1,0:T(8,128)} collective-permute-done((f32[2,64,256]{2,1,0:T(8,128)}, f32[2,64,256]{2,1,0:T(8,128)}, u32[]{:S(2)}, u32[]{:S(2)}) %collective-permute-start.18) | collective-permute-done | bytes 131104 | tf_op jit(solution)/shard_map/ppermute | solution.py:144
  192.2 1.6 copy-done
  193.8 2.5 %shard_map.81 = f32[2,1024,256]{2,1,0:T(8,128)} custom-call(s32[1]{0:T(128)} %bitcast.z, f32[2,128,256]{2,1,0:T(8,128)S(1)} %maximum_select_fusion.1.refs_0_, f32[2,128,256]{2,1,0:T(8,128)S(1)} %collective-permute-done.12.refs_1_, f32[2,128,256]{2,1,0:T(8,128)} %collective-permute-done.13.refs_2_, f32[2,128,256]{2,1,0:T(8,128)S(1)} %collective-permute-done.14.refs_3_, ...), custom_call_target="tpu_custom_call" | custom-call | bytes 4194304 | tf_op jit(solution)/shard_map/pallas_call | solution.py:202
  (48 shorter events, 1.3 us)
Async XLA Ops:
  0.6 40.5 %copy-start.3 = (s32[2,64]{1,0:T(2,128)S(1)}, s32[2,64]{1,0:T(2,128)}, u32[]{:S(2)}) copy-start(s32[2,64]{1,0:T(2,128)} %pattern.3) | copy-start | bytes 1540
  0.6 40.5 %copy-start.4 = (s32[2]{0:T(128)S(1)}, s32[2]{0:T(128)}, u32[]{:S(2)}) copy-start(s32[2]{0:T(128)} %slots.1) | copy-start | bytes 28
  0.7 40.5 %all-to-all-start = ((f32[16,64,256]{2,1,0:T(8,128)}), f32[16,64,256]{2,1,0:T(8,128)S(1)}, u32[]{:S(2)}, u32[]{:S(2)}) async-start(f32[16,64,256]{2,1,0:T(8,128)} %bitcast.19), calls=%async_computation | async-start | bytes 2097152 | tf_op jit(solution)/shard_map/all_to_all | solution.py:165
  41.7 6.6 %collective-permute-start = (f32[64,512]{1,0:T(8,128)S(1)}, f32[64,512]{1,0:T(8,128)S(1)}, u32[]{:S(2)}, u32[]{:S(2)}) collective-permute-start(f32[64,512]{1,0:T(8,128)S(1)} %shard_map.76), channel_id=1, source_target_pairs={{0,1},{1,0},{2,3},{3,2},{4,5},{5,4},{6,7},{7,6},{8,9},{9,8},{10,11... | collective-permute-start | bytes 393224 | tf_op jit(solution)/shard_map/ppermute | solution.py:170
  48.3 9.0 %collective-permute-start.4 = (f32[128,512]{1,0:T(8,128)S(1)}, f32[128,512]{1,0:T(8,128)S(1)}, u32[]{:S(2)}, u32[]{:S(2)}) collective-permute-start(f32[128,512]{1,0:T(8,128)S(1)} %bitcast.16), channel_id=1, source_target_pairs={{0,14},{2,0},{4,2},{6,4},{8,6},{10,8},{12,10},{14,12},{1,15},{3,1}... | collective-permute-start | bytes 786440 | tf_op jit(solution)/shard_map/ppermute | solution.py:143
  48.4 8.9 %collective-permute-start.1 = (f32[128,512]{1,0:T(8,128)S(1)}, f32[128,512]{1,0:T(8,128)S(1)}, u32[]{:S(2)}, u32[]{:S(2)}) collective-permute-start(f32[128,512]{1,0:T(8,128)S(1)} %bitcast.17), channel_id=1, source_target_pairs={{0,2},{2,4},{4,6},{6,8},{8,10},{10,12},{12,14},{14,0},{1,3},{3,5},... | collective-permute-start | bytes 786440 | tf_op jit(solution)/shard_map/ppermute | solution.py:142
  57.3 8.5 %collective-permute-start.5 = (f32[128,512]{1,0:T(8,128)S(1)}, f32[128,512]{1,0:T(8,128)S(1)}, u32[]{:S(2)}, u32[]{:S(2)}) collective-permute-start(f32[128,512]{1,0:T(8,128)S(1)} %collective-permute-done.4), channel_id=1, source_target_pairs={{0,14},{2,0},{4,2},{6,4},{8,6},{10,8},{12,10},{14,12},{1,15},{3,1}... | collective-permute-start | bytes 786440 | tf_op jit(solution)/shard_map/ppermute | solution.py:143
  57.3 10.1 %collective-permute-start.2 = (f32[128,512]{1,0:T(8,128)S(1)}, f32[128,512]{1,0:T(8,128)S(1)}, u32[]{:S(2)}, u32[]{:S(2)}) collective-permute-start(f32[128,512]{1,0:T(8,128)S(1)} %collective-permute-done.1), channel_id=1, source_target_pairs={{0,2},{2,4},{4,6},{6,8},{8,10},{10,12},{12,14},{14,0},{1,3},{3,5},... | collective-permute-start | bytes 786440 | tf_op jit(solution)/shard_map/ppermute | solution.py:142
  65.7 6.4 %collective-permute-start.6 = (f32[128,512]{1,0:T(8,128)S(1)}, f32[128,512]{1,0:T(8,128)S(1)}, u32[]{:S(2)}, u32[]{:S(2)}) collective-permute-start(f32[128,512]{1,0:T(8,128)S(1)} %collective-permute-done.5), channel_id=1, source_target_pairs={{0,14},{2,0},{4,2},{6,4},{8,6},{10,8},{12,10},{14,12},{1,15},{3,1}... | collective-permute-start | bytes 786440 | tf_op jit(solution)/shard_map/ppermute | solution.py:143
  67.4 8.3 %collective-permute-start.3 = (f32[128,512]{1,0:T(8,128)S(1)}, f32[128,512]{1,0:T(8,128)S(1)}, u32[]{:S(2)}, u32[]{:S(2)}) collective-permute-start(f32[128,512]{1,0:T(8,128)S(1)} %collective-permute-done.2), channel_id=1, source_target_pairs={{0,2},{2,4},{4,6},{6,8},{8,10},{10,12},{12,14},{14,0},{1,3},{3,5},... | collective-permute-start | bytes 786440 | tf_op jit(solution)/shard_map/ppermute | solution.py:142
  68.1 13.9 %copy-start.1 = (f32[1024,1024]{1,0:T(8,128)S(1)}, f32[1024,1024]{1,0:T(8,128)}, u32[]{:S(2)}) copy-start(f32[1024,1024]{1,0:T(8,128)} %left.1) | copy-start | bytes 12582916
  72.1 9.9 %collective-permute-start.8 = (f32[64,512]{1,0:T(8,128)S(1)}, f32[64,512]{1,0:T(8,128)S(1)}, u32[]{:S(2)}, u32[]{:S(2)}) collective-permute-start(f32[64,512]{1,0:T(8,128)S(1)} %slice.17), channel_id=1, source_target_pairs={{0,14},{2,0},{4,2},{6,4},{8,6},{10,8},{12,10},{14,12},{1,15},{3,1}... | collective-permute-start | bytes 393224 | tf_op jit(solution)/shard_map/ppermute | solution.py:145
  75.7 6.3 %collective-permute-start.7 = (f32[64,512]{1,0:T(8,128)S(1)}, f32[64,512]{1,0:T(8,128)S(1)}, u32[]{:S(2)}, u32[]{:S(2)}) collective-permute-start(f32[64,512]{1,0:T(8,128)S(1)} %slice.16), channel_id=1, source_target_pairs={{0,2},{2,4},{4,6},{6,8},{8,10},{10,12},{12,14},{14,0},{1,3},{3,5},... | collective-permute-start | bytes 393224 | tf_op jit(solution)/shard_map/ppermute | solution.py:144
  84.8 2.7 %collective-permute-start.9 = (f32[1024,256]{1,0:T(8,128)S(1)}, f32[1024,256]{1,0:T(8,128)S(1)}, u32[]{:S(2)}, u32[]{:S(2)}) collective-permute-start(f32[1024,256]{1,0:T(8,128)S(1)} %get-tuple-element.10), channel_id=1, source_target_pairs={{0,16},{16,0},{1,17},{17,1},{2,18},{18,2},{3,19},{19,3},{4,20},{20... | collective-permute-start | bytes 3145736 | tf_op jit(solution)/shard_map/ppermute | solution.py:174
  88.6 21.0 %all-to-all-start.1 = ((f32[8,128,256]{2,1,0:T(8,128)}), f32[8,128,256]{2,1,0:T(8,128)S(1)}, u32[]{:S(2)}, u32[]{:S(2)}) async-start(f32[8,128,256]{2,1,0:T(8,128)} %bitcast.15), calls=%async_computation.1 | async-start | bytes 2097152 | tf_op jit(solution)/shard_map/all_to_all | solution.py:176
  111.3 27.5 %all-to-all-start.2 = ((f32[8,256,128]{2,1,0:T(8,128)}), f32[8,256,128]{2,1,0:T(8,128)S(1)}, u32[]{:S(2)}, u32[]{:S(2)}) async-start(f32[8,256,128]{2,1,0:T(8,128)} %broadcast_in_dim.36), calls=%async_computation.2 | async-start | bytes 2097152 | tf_op jit(solution)/shard_map/all_to_all | solution.py:196
  116.0 14.3 %collective-permute-start.10 = (f32[128,256]{1,0:T(8,128)S(1)}, f32[128,256]{1,0:T(8,128)S(1)}, u32[]{:S(2)}, u32[]{:S(2)}) collective-permute-start(f32[128,256]{1,0:T(8,128)S(1)} %get-tuple-element.11), channel_id=1, source_target_pairs={{0,0},{1,16},{2,32},{3,48},{4,64},{5,80},{6,96},{7,112},{8,128},{9... | collective-permute-start | bytes 393224 | tf_op jit(solution)/shard_map/ppermute | solution.py:181
  130.4 17.0 %collective-permute-start.11 = (f32[128,256]{1,0:T(8,128)S(1)}, f32[128,256]{1,0:T(8,128)}, u32[]{:S(2)}, u32[]{:S(2)}) collective-permute-start(f32[128,256]{1,0:T(8,128)S(1)} %collective-permute-done.10.right), channel_id=1, source_target_pairs={{0,1},{1,0},{2,3},{3,2},{4,5},{5,4},{6,7},{7,6},{8,9},{9,8},{10,11... | collective-permute-start | bytes 393224 | tf_op jit(solution)/shard_map/ppermute | solution.py:182
  138.8 47.9 %collective-permute-start.20 = (f32[8,256,128]{2,1,0:T(8,128)S(1)}, f32[8,256,128]{2,1,0:T(8,128)}, u32[]{:S(2)}, u32[]{:S(2)}) collective-permute-start(f32[8,256,128]{2,1,0:T(8,128)S(1)} %all-to-all-done.2.mine), channel_id=1, source_target_pairs={{0,16},{16,0},{1,17},{17,1},{2,18},{18,2},{3,19},{19,3},{4,20},{20... | collective-permute-start | bytes 3145736 | tf_op jit(solution)/shard_map/ppermute | solution.py:197
  140.5 45.4 %copy-start.2 = (f32[2,256,256]{2,1,0:T(8,128)S(1)}, f32[2,256,256]{2,1,0:T(8,128)}, u32[]{:S(2)}) copy-start(f32[2,256,256]{2,1,0:T(8,128)} %given.1) | copy-start | bytes 1572868
  140.5 13.7 %all-to-all-start.3 = ((f32[16,16,256]{2,1,0:T(8,128)}), f32[16,16,256]{2,1,0:T(8,128)S(1)}, u32[]{:S(2)}, u32[]{:S(2)}) async-start(f32[16,16,256]{2,1,0:T(8,128)} %shard_map.82), calls=%async_computation.3 | async-start | bytes 524288 | tf_op jit(solution)/shard_map/all_to_all | solution.py:187
  148.4 9.9 %collective-permute-start.15 = (f32[2,128,256]{2,1,0:T(8,128)S(1)}, f32[2,128,256]{2,1,0:T(8,128)S(1)}, u32[]{:S(2)}, u32[]{:S(2)}) collective-permute-start(f32[2,128,256]{2,1,0:T(8,128)S(1)} %maximum_select_fusion.1.refs_0_), channel_id=1, source_target_pairs={{0,14},{2,0},{4,2},{6,4},{8,6},{10,8},{12,10},{14,12},{1,15},{3,1}... | collective-permute-start | bytes 786440 | tf_op jit(solution)/shard_map/ppermute | solution.py:143
  150.2 11.3 %collective-permute-start.12 = (f32[2,128,256]{2,1,0:T(8,128)S(1)}, f32[2,128,256]{2,1,0:T(8,128)S(1)}, u32[]{:S(2)}, u32[]{:S(2)}) collective-permute-start(f32[2,128,256]{2,1,0:T(8,128)S(1)} %maximum_select_fusion.1.refs_0_), channel_id=1, source_target_pairs={{0,2},{2,4},{4,6},{6,8},{8,10},{10,12},{12,14},{14,0},{1,3},{3,5},... | collective-permute-start | bytes 786440 | tf_op jit(solution)/shard_map/ppermute | solution.py:142
  154.9 13.4 %all-to-all-start.4 = ((f32[8,16,256]{2,1,0:T(8,128)}), f32[8,16,256]{2,1,0:T(8,128)S(1)}, u32[]{:S(2)}, u32[]{:S(2)}) async-start(f32[8,16,256]{2,1,0:T(8,128)} %broadcast_in_dim.37), calls=%async_computation.4 | async-start | bytes 262144 | tf_op jit(solution)/shard_map/all_to_all | solution.py:188
  158.3 15.6 %collective-permute-start.16 = (f32[2,128,256]{2,1,0:T(8,128)S(1)}, f32[2,128,256]{2,1,0:T(8,128)}, u32[]{:S(2)}, u32[]{:S(2)}) collective-permute-start(f32[2,128,256]{2,1,0:T(8,128)S(1)} %collective-permute-done.15.refs_4_), channel_id=1, source_target_pairs={{0,14},{2,0},{4,2},{6,4},{8,6},{10,8},{12,10},{14,12},{1,15},{3,1}... | collective-permute-start | bytes 786440 | tf_op jit(solution)/shard_map/ppermute | solution.py:143
  161.5 13.1 %collective-permute-start.13 = (f32[2,128,256]{2,1,0:T(8,128)S(1)}, f32[2,128,256]{2,1,0:T(8,128)}, u32[]{:S(2)}, u32[]{:S(2)}) collective-permute-start(f32[2,128,256]{2,1,0:T(8,128)S(1)} %collective-permute-done.12.refs_1_), channel_id=1, source_target_pairs={{0,2},{2,4},{4,6},{6,8},{8,10},{10,12},{12,14},{14,0},{1,3},{3,5},... | collective-permute-start | bytes 786440 | tf_op jit(solution)/shard_map/ppermute | solution.py:142
  169.1 16.7 %all-to-all-start.5 = ((f32[32,16,256]{2,1,0:T(8,128)}), f32[32,16,256]{2,1,0:T(8,128)S(1)}, u32[]{:S(2)}, u32[]{:S(2)}) async-start(f32[32,16,256]{2,1,0:T(8,128)} %broadcast_in_dim.38), calls=%async_computation.5 | async-start | bytes 1048576 | tf_op jit(solution)/shard_map/all_to_all | solution.py:191
  173.8 8.6 %collective-permute-start.17 = (f32[2,128,256]{2,1,0:T(8,128)}, f32[2,128,256]{2,1,0:T(8,128)S(1)}, u32[]{:S(2)}, u32[]{:S(2)}) collective-permute-start(f32[2,128,256]{2,1,0:T(8,128)} %collective-permute-done.16.refs_5_), channel_id=1, source_target_pairs={{0,14},{2,0},{4,2},{6,4},{8,6},{10,8},{12,10},{14,12},{1,15},{3,1}... | collective-permute-start | bytes 786440 | tf_op jit(solution)/shard_map/ppermute | solution.py:143
  174.6 10.4 %collective-permute-start.14 = (f32[2,128,256]{2,1,0:T(8,128)}, f32[2,128,256]{2,1,0:T(8,128)S(1)}, u32[]{:S(2)}, u32[]{:S(2)}) collective-permute-start(f32[2,128,256]{2,1,0:T(8,128)} %collective-permute-done.13.refs_2_), channel_id=1, source_target_pairs={{0,2},{2,4},{4,6},{6,8},{8,10},{10,12},{12,14},{14,0},{1,3},{3,5},... | collective-permute-start | bytes 786440 | tf_op jit(solution)/shard_map/ppermute | solution.py:142
  183.2 6.4 %collective-permute-start.19 = (f32[2,64,256]{2,1,0:T(8,128)}, f32[2,64,256]{2,1,0:T(8,128)S(1)}, u32[]{:S(2)}, u32[]{:S(2)}) collective-permute-start(f32[2,64,256]{2,1,0:T(8,128)} %slice.19), channel_id=1, source_target_pairs={{0,14},{2,0},{4,2},{6,4},{8,6},{10,8},{12,10},{14,12},{1,15},{3,1}... | collective-permute-start | bytes 393224 | tf_op jit(solution)/shard_map/ppermute | solution.py:145
  185.7 6.5 %collective-permute-start.18 = (f32[2,64,256]{2,1,0:T(8,128)}, f32[2,64,256]{2,1,0:T(8,128)}, u32[]{:S(2)}, u32[]{:S(2)}) collective-permute-start(f32[2,64,256]{2,1,0:T(8,128)} %slice.18), channel_id=1, source_target_pairs={{0,2},{2,4},{4,6},{6,8},{8,10},{10,12},{12,14},{14,0},{1,3},{3,5},... | collective-permute-start | bytes 393224 | tf_op jit(solution)/shard_map/ppermute | solution.py:144
  192.2 1.6 copy-start
where the time goes:
time: 197 us; the launch traced here: 196 us
  waiting for transfers between devices  115 us (58%)
  starting transfers between devices  58.1 us (29%)
  Pallas kernels  14.3 us (7%)
  local copies, waits for them, and re-layouts  5.96 us (3%)
  other arithmetic  2.32 us (1%)
    all_to_all x1, waiting for transfers between devices, shards(): lax.all_to_all(panels[0].reshape(16, 64, 256), COL, 0, 0, tiled=True)  30.2 us
    ppermute x6, waiting for transfers between devices, ring(): downs.append(lax.ppermute(downs[-1], 'z', DOWN))  23.6 us
    all_to_all x1, waiting for transfers between devices, shards(): terms = lax.all_to_all(term.reshape(8, 128, 256), CHIP, 0, 0, tiled=True)  15 us
    ppermute x1, waiting for transfers between devices, shards(): mine = lax.ppermute(column, ALL, TRANSPOSE)  12.4 us
    all_to_all x1, starting transfers between devices, shards(): lax.all_to_all(panels[0].reshape(16, 64, 256), COL, 0, 0, tiled=True)  10.3 us
    ppermute x2, waiting for transfers between devices, ring(): top = lax.ppermute(ups[-1][..., :half, :], 'z', UP)  8.66 us
    all_to_all x1, waiting for transfers between devices, shards(): turned = lax.all_to_all(turned, CHIP, 0, 0, tiled=True)  8.47 us
    ppermute x6, starting transfers between devices, ring(): downs.append(lax.ppermute(downs[-1], 'z', DOWN))  7.46 us
  transfers between devices with their start and end apart: 27, of which 14 were waited for; matrix products, arithmetic and copies ran while one was open for 2% of the time, Pallas kernels for 4%

commit v1 on v0

--- a/solution.py
+++ b/solution.py
@@ -99,18 +99,36 @@
 
 
 def inner_kernel(at, left, right, out):
-    rows = pl.ds(pl.multiple_of(at[0] * 128, 128), 128)
-    columns = pl.ds(pl.multiple_of(at[1] * 256, 256), 256)
-    inner = dot3(halves(left[rows, columns].T), halves(right[...]))
+    columns = pl.ds(pl.multiple_of(at[0] * 256, 256), 256)
+    inner = dot3(halves(left[:, columns].T), halves(right[...]))
     for k in range(16):
         out[k] = inner[k * 16 : k * 16 + 16]
 
 
-def rows_kernel(core, mine, other, out):
+def rows_kernel(core, mine, other, out, done):
     for k in range(8):
         columns = slice(k * 128, k * 128 + 128)
         out[core[0], :, columns] = mine[k]
         out[1 - core[0], :, columns] = other[k]
+    done[...] = mine[0, :8]
+
+
+def add_kernel(pieces, out):
+    total = pieces[0]
+    for k in range(1, pieces.shape[0]):
+        total += pieces[k]
+    for k in range(out.shape[0]):
+        out[k] = total
+
+
+def add_up(pieces, receivers):
+    out = ((receivers, 16, 256), jnp.float32)
+    return call(add_kernel, [out], [VMEM], [VMEM], nbytes=1 << 19)(pieces)
+
+
+def pair_kernel(xh, mine, other, out):
+    out[xh[0]] = mine[...]
+    out[1 - xh[0]] = other[...]
 
 
 def diag_kernel(given, pieces, out):
@@ -179,15 +197,14 @@
     column, turned = call(reduce_kernel, outs, [SMEM, SMEM, VMEM], [VMEM, VMEM])(at, pattern, terms)
 
     mine = lax.ppermute(column, ALL, TRANSPOSE)
-    pieces = ring(both(mine, lax.ppermute(mine, "xh", SWAP), xh == 0))
+    other = lax.ppermute(mine, "xh", SWAP)
+    out = ((2, 128, 256), jnp.float32)
+    pieces = ring(call(pair_kernel, [out], [SMEM, VMEM, VMEM], [VMEM], nbytes=1 << 19)(xh[None], mine, other))
 
     out = ((16, 16, 256), jnp.float32)
-    at = jnp.stack([z, xh])
-    inner = call(inner_kernel, [out], [SMEM, VMEM, VMEM], [VMEM], flops=3 << 24)(at, masked, mine)
-    inner = jnp.sum(lax.all_to_all(inner, ROW, 0, 0, tiled=True), axis=0)
-    inner = lax.all_to_all(jnp.broadcast_to(inner[None], (8, 16, 256)), "z", 0, 0, tiled=True)
-    inner = jnp.sum(inner, axis=0)
-    inner = jnp.broadcast_to(inner[None], (32, 16, 256))
+    inner = call(inner_kernel, [out], [SMEM, VMEM, VMEM], [VMEM], flops=3 << 24)(xh[None], block, mine)
+    inner = add_up(lax.all_to_all(inner, ROW, 0, 0, tiled=True), 8)
+    inner = add_up(lax.all_to_all(inner, "z", 0, 0, tiled=True), 32)
     inner = lax.all_to_all(inner, ROW + ("xh",), 0, 0, tiled=True)
     out = ((2, 256, 256), jnp.float32)
     diag = call(diag_kernel, [out], [VMEM, VMEM], [VMEM], nbytes=3 << 19)(diag_inverse, inner)
@@ -195,12 +212,12 @@
     turned = jnp.broadcast_to(turned[None], (8, 256, 128))
     turned = lax.all_to_all(turned, CHIP, 0, 0, tiled=True)
     other = lax.ppermute(turned, "core", SWAP)
-    out = ((2, 256, 1024), jnp.float32)
-    rows = call(rows_kernel, [out], [SMEM, VMEM, VMEM], [VMEM], nbytes=1 << 22)(core[None], turned, other)
+    outs = [((2, 256, 1024), jnp.float32), ((8, 128), jnp.float32)]
+    rows, done = call(rows_kernel, outs, [SMEM, VMEM, VMEM], [VMEM] * 2, nbytes=1 << 22)(core[None], turned, other)
 
     out = ((2, 1024, 256), jnp.float32)
     lower = call(place_kernel, [out], [SMEM] + [VMEM] * 9 + [ANY], [VMEM], nbytes=1 << 22)(
-        z[None], *pieces, rows
+        z[None], *pieces, done
     )
     return lower, rows, diag
 

time: 197 us -> 195 us (0.990)
  local copies, waits for them, and re-layouts: 5.96 us -> 3.91 us
  transfers between devices with their start and end apart: 27 -> 27, of which waited for: 14 -> 14; matrix products, arithmetic and copies ran while one was open for 2% -> 1% of each run, Pallas kernels for 4% -> 4%
where the time goes in v1:
time: 195 us; the launch traced here: 194 us
  waiting for transfers between devices  116 us (59%)
  starting transfers between devices  58 us (30%)
  Pallas kernels  14.1 us (7%)
  local copies, waits for them, and re-layouts  3.91 us (2%)
    all_to_all x1, waiting for transfers between devices, shards(): lax.all_to_all(panels[0].reshape(16, 64, 256), COL, 0, 0, tiled=True)  30.1 us
    ppermute x6, waiting for transfers between devices, ring(): downs.append(lax.ppermute(downs[-1], 'z', DOWN))  23.6 us
    all_to_all x1, waiting for transfers between devices, shards(): terms = lax.all_to_all(term.reshape(8, 128, 256), CHIP, 0, 0, tiled=True)  15 us
    ppermute x1, waiting for transfers between devices, shards(): mine = lax.ppermute(column, ALL, TRANSPOSE)  12.4 us
    all_to_all x1, starting transfers between devices, shards(): lax.all_to_all(panels[0].reshape(16, 64, 256), COL, 0, 0, tiled=True)  10.3 us
    ppermute x2, waiting for transfers between devices, ring(): top = lax.ppermute(ups[-1][..., :half, :], 'z', UP)  8.91 us
    all_to_all x1, waiting for transfers between devices, shards(): turned = lax.all_to_all(turned, CHIP, 0, 0, tiled=True)  8.47 us
    ppermute x6, starting transfers between devices, ring(): downs.append(lax.ppermute(downs[-1], 'z', DOWN))  7.59 us
  transfers between devices with their start and end apart: 27, of which 14 were waited for; matrix products, arithmetic and copies ran while one was open for 1% of the time, Pallas kernels for 4%

profile of v1, /device:TPU:2, one launch (start us, length us, event | category | flops | bytes accessed | tf_op | source)
XLA Modules:
  0.0 194.0 jit_solution(12040134804361931962)
XLA Ops:
  0.7 10.3 %all-to-all-start = ((f32[16,64,256]{2,1,0:T(8,128)}), f32[16,64,256]{2,1,0:T(8,128)S(1)}, u32[]{:S(2)}, u32[]{:S(2)}) async-start(f32[16,64,256]{2,1,0:T(8,128)} %bitcast.16), calls=%async_computation | async-start | bytes 2097152 | tf_op jit(solution)/shard_map/all_to_all | solution.py:183
  11.0 30.1 %all-to-all-done.dealt = f32[16,64,256]{2,1,0:T(8,128)S(1)} async-done(((f32[16,64,256]{2,1,0:T(8,128)}), f32[16,64,256]{2,1,0:T(8,128)S(1)}, u32[]{:S(2)}, u32[]{:S(2)}) %all-to-all-start) | async-done | bytes 1048608 | tf_op jit(solution)/shard_map/all_to_all | solution.py:183
  41.1 0.6 shard_map.76
  41.7 0.5 collective-permute-start
  42.2 6.0 %collective-permute-done = f32[64,512]{1,0:T(8,128)S(1)} collective-permute-done((f32[64,512]{1,0:T(8,128)S(1)}, f32[64,512]{1,0:T(8,128)S(1)}, u32[]{:S(2)}, u32[]{:S(2)}) %collective-permute-start) | collective-permute-done | bytes 131104 | tf_op jit(solution)/shard_map/ppermute | solution.py:188
  48.4 2.0 %collective-permute-start.1 = (f32[128,512]{1,0:T(8,128)S(1)}, f32[128,512]{1,0:T(8,128)S(1)}, u32[]{:S(2)}, u32[]{:S(2)}) collective-permute-start(f32[128,512]{1,0:T(8,128)S(1)} %bitcast.12), channel_id=1, source_target_pairs={{0,2},{2,4},{4,6},{6,8},{8,10},{10,12},{12,14},{14,0},{1,3},{3,5},... | collective-permute-start | bytes 786440 | tf_op jit(solution)/shard_map/ppermute | solution.py:160
  50.4 6.9 %collective-permute-done.4 = f32[128,512]{1,0:T(8,128)S(1)} collective-permute-done((f32[128,512]{1,0:T(8,128)S(1)}, f32[128,512]{1,0:T(8,128)S(1)}, u32[]{:S(2)}, u32[]{:S(2)}) %collective-permute-start.4) | collective-permute-done | bytes 262176 | tf_op jit(solution)/shard_map/ppermute | solution.py:161
  57.3 2.2 %collective-permute-start.2 = (f32[128,512]{1,0:T(8,128)S(1)}, f32[128,512]{1,0:T(8,128)S(1)}, u32[]{:S(2)}, u32[]{:S(2)}) collective-permute-start(f32[128,512]{1,0:T(8,128)S(1)} %collective-permute-done.1), channel_id=1, source_target_pairs={{0,2},{2,4},{4,6},{6,8},{8,10},{10,12},{12,14},{14,0},{1,3},{3,5},... | collective-permute-start | bytes 786440 | tf_op jit(solution)/shard_map/ppermute | solution.py:160
  59.5 6.2 %collective-permute-done.5 = f32[128,512]{1,0:T(8,128)S(1)} collective-permute-done((f32[128,512]{1,0:T(8,128)S(1)}, f32[128,512]{1,0:T(8,128)S(1)}, u32[]{:S(2)}, u32[]{:S(2)}) %collective-permute-start.5) | collective-permute-done | bytes 262176 | tf_op jit(solution)/shard_map/ppermute | solution.py:161
  65.7 1.6 collective-permute-start.6
  67.4 0.4 collective-permute-start.3
  67.8 0.2 broadcast_in_dim.27
  68.2 3.9 %collective-permute-done.6 = f32[128,512]{1,0:T(8,128)S(1)} collective-permute-done((f32[128,512]{1,0:T(8,128)S(1)}, f32[128,512]{1,0:T(8,128)S(1)}, u32[]{:S(2)}, u32[]{:S(2)}) %collective-permute-start.6) | collective-permute-done | bytes 262176 | tf_op jit(solution)/shard_map/ppermute | solution.py:161
  72.1 3.6 %collective-permute-start.8 = (f32[64,512]{1,0:T(8,128)S(1)}, f32[64,512]{1,0:T(8,128)S(1)}, u32[]{:S(2)}, u32[]{:S(2)}) collective-permute-start(f32[64,512]{1,0:T(8,128)S(1)} %slice.17), channel_id=1, source_target_pairs={{0,14},{2,0},{4,2},{6,4},{8,6},{10,8},{12,10},{14,12},{1,15},{3,1}... | collective-permute-start | bytes 393224 | tf_op jit(solution)/shard_map/ppermute | solution.py:163
  75.9 6.0 %collective-permute-done.7 = f32[64,512]{1,0:T(8,128)S(1)} collective-permute-done((f32[64,512]{1,0:T(8,128)S(1)}, f32[64,512]{1,0:T(8,128)S(1)}, u32[]{:S(2)}, u32[]{:S(2)}) %collective-permute-start.7) | collective-permute-done | bytes 131104 | tf_op jit(solution)/shard_map/ppermute | solution.py:162
  82.0 2.7 %shard_map.77 = (f32[1024,256]{1,0:T(8,128)S(1)}, bf16[1024,1024]{1,0:T(8,128)(2,1)S(1)}, bf16[1024,1024]{1,0:T(8,128)(2,1)S(1)}) custom-call(s32[1]{0:T(128)} %bitcast.4.number, f32[1024,1024]{1,0:T(8,128)S(1)} %copy-done, f32[1024,512]{1,0:T(8,128)S(1)} %constant_dynamic-update-slice_fusion.right), custom_call_target="tpu_custom_call" | custom-call | flops 1610612736 | bytes 7340032 | tf_op jit(solution)/shard_map/pallas_call | solution.py:82
  84.9 2.5 %shard_map.78 = f32[1024,256]{1,0:T(8,128)S(1)} custom-call(s32[1]{0:T(128)} %bitcast.2.number.core, bf16[1024,1024]{1,0:T(8,128)(2,1)S(1)} %get-tuple-element.10.high, bf16[1024,1024]{1,0:T(8,128)(2,1)S(1)} %get-tuple-element.11.low, f32[1024,512]{1,0:T(8,128)S(1)} %constant_dynamic-update-slice_fusion.right), custom_call_target="tpu_custom_call" | custom-call | flops 1610612736 | bytes 7340032 | tf_op jit(solution)/shard_map/pallas_call | solution.py:83
  87.5 1.1 add.134
  88.6 5.9 %all-to-all-start.1 = ((f32[8,128,256]{2,1,0:T(8,128)}), f32[8,128,256]{2,1,0:T(8,128)S(1)}, u32[]{:S(2)}, u32[]{:S(2)}) async-start(f32[8,128,256]{2,1,0:T(8,128)} %bitcast.10), calls=%async_computation.1 | async-start | bytes 2097152 | tf_op jit(solution)/shard_map/all_to_all | solution.py:194
  94.6 15.0 %all-to-all-done.1.terms = f32[8,128,256]{2,1,0:T(8,128)S(1)} async-done(((f32[8,128,256]{2,1,0:T(8,128)}), f32[8,128,256]{2,1,0:T(8,128)S(1)}, u32[]{:S(2)}, u32[]{:S(2)}) %all-to-all-start.1) | async-done | bytes 1048608 | tf_op jit(solution)/shard_map/all_to_all | solution.py:194
  109.6 0.7 shard_map.79
  110.3 1.0 broadcast_in_dim.29
  111.3 4.7 %all-to-all-start.2 = ((f32[8,256,128]{2,1,0:T(8,128)}), f32[8,256,128]{2,1,0:T(8,128)S(1)}, u32[]{:S(2)}, u32[]{:S(2)}) async-start(f32[8,256,128]{2,1,0:T(8,128)} %broadcast_in_dim.29), calls=%async_computation.2 | async-start | bytes 2097152 | tf_op jit(solution)/shard_map/all_to_all | solution.py:213
  116.0 1.9 collective-permute-start.10
  117.9 12.4 %collective-permute-done.10.mine.right = f32[128,256]{1,0:T(8,128)S(1)} collective-permute-done((f32[128,256]{1,0:T(8,128)S(1)}, f32[128,256]{1,0:T(8,128)S(1)}, u32[]{:S(2)}, u32[]{:S(2)}) %collective-permute-start.10) | collective-permute-done | bytes 131104 | tf_op jit(solution)/shard_map/ppermute | solution.py:199
  130.4 8.5 %all-to-all-done.2.mine = f32[8,256,128]{2,1,0:T(8,128)S(1)} async-done(((f32[8,256,128]{2,1,0:T(8,128)}), f32[8,256,128]{2,1,0:T(8,128)S(1)}, u32[]{:S(2)}, u32[]{:S(2)}) %all-to-all-start.2) | async-done | bytes 1048608 | tf_op jit(solution)/shard_map/all_to_all | solution.py:213
  138.8 1.0 shard_map.83
  139.9 6.8 %all-to-all-start.3 = ((f32[16,16,256]{2,1,0:T(8,128)}), f32[16,16,256]{2,1,0:T(8,128)S(1)}, u32[]{:S(2)}, u32[]{:S(2)}) async-start(f32[16,16,256]{2,1,0:T(8,128)} %shard_map.83), calls=%async_computation.3 | async-start | bytes 524288 | tf_op jit(solution)/shard_map/all_to_all | solution.py:206
  146.7 1.8 collective-permute-start.15
  148.5 0.5 collective-permute-start.12
  148.9 4.5 %all-to-all-done.3.pieces = f32[16,16,256]{2,1,0:T(8,128)S(1)} async-done(((f32[16,16,256]{2,1,0:T(8,128)}), f32[16,16,256]{2,1,0:T(8,128)S(1)}, u32[]{:S(2)}, u32[]{:S(2)}) %all-to-all-start.3) | async-done | bytes 262176 | tf_op jit(solution)/shard_map/all_to_all | solution.py:206
  153.4 0.7 shard_map.84
  154.1 3.4 %all-to-all-start.4 = ((f32[8,16,256]{2,1,0:T(8,128)}), f32[8,16,256]{2,1,0:T(8,128)S(1)}, u32[]{:S(2)}, u32[]{:S(2)}) async-start(f32[8,16,256]{2,1,0:T(8,128)} %shard_map.84), calls=%async_computation.4 | async-start | bytes 262144 | tf_op jit(solution)/shard_map/all_to_all | solution.py:207
  157.5 3.3 %collective-permute-start.16 = (f32[2,128,256]{2,1,0:T(8,128)S(1)}, f32[2,128,256]{2,1,0:T(8,128)}, u32[]{:S(2)}, u32[]{:S(2)}) collective-permute-start(f32[2,128,256]{2,1,0:T(8,128)S(1)} %collective-permute-done.15.refs_4_), channel_id=1, source_target_pairs={{0,14},{2,0},{4,2},{6,4},{8,6},{10,8},{12,10},{14,12},{1,15},{3,1}... | collective-permute-start | bytes 786440 | tf_op jit(solution)/shard_map/ppermute | solution.py:161
  160.8 6.7 %all-to-all-done.4.pieces = f32[8,16,256]{2,1,0:T(8,128)S(1)} async-done(((f32[8,16,256]{2,1,0:T(8,128)}), f32[8,16,256]{2,1,0:T(8,128)S(1)}, u32[]{:S(2)}, u32[]{:S(2)}) %all-to-all-start.4) | async-done | bytes 131104 | tf_op jit(solution)/shard_map/all_to_all | solution.py:207
  167.5 0.9 shard_map.85
  168.4 4.7 %all-to-all-start.5 = ((f32[32,16,256]{2,1,0:T(8,128)}), f32[32,16,256]{2,1,0:T(8,128)S(1)}, u32[]{:S(2)}, u32[]{:S(2)}) async-start(f32[32,16,256]{2,1,0:T(8,128)} %shard_map.85), calls=%async_computation.5 | async-start | bytes 1048576 | tf_op jit(solution)/shard_map/all_to_all | solution.py:208
  173.1 0.8 collective-permute-start.17
  173.9 1.3 collective-permute-start.14
  175.2 6.5 %collective-permute-done.17.refs_6_ = f32[2,128,256]{2,1,0:T(8,128)S(1)} collective-permute-done((f32[2,128,256]{2,1,0:T(8,128)}, f32[2,128,256]{2,1,0:T(8,128)S(1)}, u32[]{:S(2)}, u32[]{:S(2)}) %collective-permute-start.17) | collective-permute-done | bytes 262176 | tf_op jit(solution)/shard_map/ppermute | solution.py:161
  181.7 0.7 slice.19
  182.4 1.9 collective-permute-start.19
  184.3 0.7 slice.18
  185.1 1.0 copy-done.1
  186.1 0.8 shard_map.86
  187.0 1.6 shard_map.81
  188.6 2.9 %collective-permute-done.18.refs_7_ = f32[2,64,256]{2,1,0:T(8,128)} collective-permute-done((f32[2,64,256]{2,1,0:T(8,128)}, f32[2,64,256]{2,1,0:T(8,128)}, u32[]{:S(2)}, u32[]{:S(2)}) %collective-permute-start.18) | collective-permute-done | bytes 131104 | tf_op jit(solution)/shard_map/ppermute | solution.py:162
  191.5 2.5 %shard_map.82 = f32[2,1024,256]{2,1,0:T(8,128)} custom-call(s32[1]{0:T(128)} %bitcast.z, f32[2,128,256]{2,1,0:T(8,128)S(1)} %shard_map.80.refs_0_, f32[2,128,256]{2,1,0:T(8,128)S(1)} %copy-done.5, f32[2,128,256]{2,1,0:T(8,128)} %collective-permute-done.13.refs_2_, f32[2,128,256]{2,1,0:T(8,128)S(1)} %collective-permute-done.14.refs_3_, ...), custom_call_target="tpu_custom_call" | custom-call | bytes 4194304 | tf_op jit(solution)/shard_map/pallas_call | solution.py:219
  (51 shorter events, 0.9 us)
Async XLA Ops:
  0.6 40.5 %copy-start.6 = (s32[2,64]{1,0:T(2,128)S(1)}, s32[2,64]{1,0:T(2,128)}, u32[]{:S(2)}) copy-start(s32[2,64]{1,0:T(2,128)} %pattern.3) | copy-start | bytes 1540
  0.6 40.5 %copy-start.7 = (s32[2]{0:T(128)S(1)}, s32[2]{0:T(128)}, u32[]{:S(2)}) copy-start(s32[2]{0:T(128)} %slots.1) | copy-start | bytes 28
  0.7 40.5 %all-to-all-start = ((f32[16,64,256]{2,1,0:T(8,128)}), f32[16,64,256]{2,1,0:T(8,128)S(1)}, u32[]{:S(2)}, u32[]{:S(2)}) async-start(f32[16,64,256]{2,1,0:T(8,128)} %bitcast.16), calls=%async_computation | async-start | bytes 2097152 | tf_op jit(solution)/shard_map/all_to_all | solution.py:183
  41.7 6.6 %collective-permute-start = (f32[64,512]{1,0:T(8,128)S(1)}, f32[64,512]{1,0:T(8,128)S(1)}, u32[]{:S(2)}, u32[]{:S(2)}) collective-permute-start(f32[64,512]{1,0:T(8,128)S(1)} %shard_map.76), channel_id=1, source_target_pairs={{0,1},{1,0},{2,3},{3,2},{4,5},{5,4},{6,7},{7,6},{8,9},{9,8},{10,11... | collective-permute-start | bytes 393224 | tf_op jit(solution)/shard_map/ppermute | solution.py:188
  48.3 9.0 %collective-permute-start.4 = (f32[128,512]{1,0:T(8,128)S(1)}, f32[128,512]{1,0:T(8,128)S(1)}, u32[]{:S(2)}, u32[]{:S(2)}) collective-permute-start(f32[128,512]{1,0:T(8,128)S(1)} %bitcast.11), channel_id=1, source_target_pairs={{0,14},{2,0},{4,2},{6,4},{8,6},{10,8},{12,10},{14,12},{1,15},{3,1}... | collective-permute-start | bytes 786440 | tf_op jit(solution)/shard_map/ppermute | solution.py:161
  48.4 8.9 %collective-permute-start.1 = (f32[128,512]{1,0:T(8,128)S(1)}, f32[128,512]{1,0:T(8,128)S(1)}, u32[]{:S(2)}, u32[]{:S(2)}) collective-permute-start(f32[128,512]{1,0:T(8,128)S(1)} %bitcast.12), channel_id=1, source_target_pairs={{0,2},{2,4},{4,6},{6,8},{8,10},{10,12},{12,14},{14,0},{1,3},{3,5},... | collective-permute-start | bytes 786440 | tf_op jit(solution)/shard_map/ppermute | solution.py:160
  57.3 8.5 %collective-permute-start.5 = (f32[128,512]{1,0:T(8,128)S(1)}, f32[128,512]{1,0:T(8,128)S(1)}, u32[]{:S(2)}, u32[]{:S(2)}) collective-permute-start(f32[128,512]{1,0:T(8,128)S(1)} %collective-permute-done.4), channel_id=1, source_target_pairs={{0,14},{2,0},{4,2},{6,4},{8,6},{10,8},{12,10},{14,12},{1,15},{3,1}... | collective-permute-start | bytes 786440 | tf_op jit(solution)/shard_map/ppermute | solution.py:161
  57.3 10.1 %collective-permute-start.2 = (f32[128,512]{1,0:T(8,128)S(1)}, f32[128,512]{1,0:T(8,128)S(1)}, u32[]{:S(2)}, u32[]{:S(2)}) collective-permute-start(f32[128,512]{1,0:T(8,128)S(1)} %collective-permute-done.1), channel_id=1, source_target_pairs={{0,2},{2,4},{4,6},{6,8},{8,10},{10,12},{12,14},{14,0},{1,3},{3,5},... | collective-permute-start | bytes 786440 | tf_op jit(solution)/shard_map/ppermute | solution.py:160
  65.7 6.4 %collective-permute-start.6 = (f32[128,512]{1,0:T(8,128)S(1)}, f32[128,512]{1,0:T(8,128)S(1)}, u32[]{:S(2)}, u32[]{:S(2)}) collective-permute-start(f32[128,512]{1,0:T(8,128)S(1)} %collective-permute-done.5), channel_id=1, source_target_pairs={{0,14},{2,0},{4,2},{6,4},{8,6},{10,8},{12,10},{14,12},{1,15},{3,1}... | collective-permute-start | bytes 786440 | tf_op jit(solution)/shard_map/ppermute | solution.py:161
  67.4 8.3 %collective-permute-start.3 = (f32[128,512]{1,0:T(8,128)S(1)}, f32[128,512]{1,0:T(8,128)S(1)}, u32[]{:S(2)}, u32[]{:S(2)}) collective-permute-start(f32[128,512]{1,0:T(8,128)S(1)} %collective-permute-done.2), channel_id=1, source_target_pairs={{0,2},{2,4},{4,6},{6,8},{8,10},{10,12},{12,14},{14,0},{1,3},{3,5},... | collective-permute-start | bytes 786440 | tf_op jit(solution)/shard_map/ppermute | solution.py:160
  68.1 13.9 %copy-start = (f32[1024,1024]{1,0:T(8,128)S(1)}, f32[1024,1024]{1,0:T(8,128)}, u32[]{:S(2)}) copy-start(f32[1024,1024]{1,0:T(8,128)} %left.1) | copy-start | bytes 12582916
  72.1 9.9 %collective-permute-start.8 = (f32[64,512]{1,0:T(8,128)S(1)}, f32[64,512]{1,0:T(8,128)S(1)}, u32[]{:S(2)}, u32[]{:S(2)}) collective-permute-start(f32[64,512]{1,0:T(8,128)S(1)} %slice.17), channel_id=1, source_target_pairs={{0,14},{2,0},{4,2},{6,4},{8,6},{10,8},{12,10},{14,12},{1,15},{3,1}... | collective-permute-start | bytes 393224 | tf_op jit(solution)/shard_map/ppermute | solution.py:163
  75.7 6.3 %collective-permute-start.7 = (f32[64,512]{1,0:T(8,128)S(1)}, f32[64,512]{1,0:T(8,128)S(1)}, u32[]{:S(2)}, u32[]{:S(2)}) collective-permute-start(f32[64,512]{1,0:T(8,128)S(1)} %slice.16), channel_id=1, source_target_pairs={{0,2},{2,4},{4,6},{6,8},{8,10},{10,12},{12,14},{14,0},{1,3},{3,5},... | collective-permute-start | bytes 393224 | tf_op jit(solution)/shard_map/ppermute | solution.py:162
  84.8 2.7 %collective-permute-start.9 = (f32[1024,256]{1,0:T(8,128)S(1)}, f32[1024,256]{1,0:T(8,128)S(1)}, u32[]{:S(2)}, u32[]{:S(2)}) collective-permute-start(f32[1024,256]{1,0:T(8,128)S(1)} %get-tuple-element.12), channel_id=1, source_target_pairs={{0,16},{16,0},{1,17},{17,1},{2,18},{18,2},{3,19},{19,3},{4,20},{20... | collective-permute-start | bytes 3145736 | tf_op jit(solution)/shard_map/ppermute | solution.py:192
  88.6 21.0 %all-to-all-start.1 = ((f32[8,128,256]{2,1,0:T(8,128)}), f32[8,128,256]{2,1,0:T(8,128)S(1)}, u32[]{:S(2)}, u32[]{:S(2)}) async-start(f32[8,128,256]{2,1,0:T(8,128)} %bitcast.10), calls=%async_computation.1 | async-start | bytes 2097152 | tf_op jit(solution)/shard_map/all_to_all | solution.py:194
  111.3 27.5 %all-to-all-start.2 = ((f32[8,256,128]{2,1,0:T(8,128)}), f32[8,256,128]{2,1,0:T(8,128)S(1)}, u32[]{:S(2)}, u32[]{:S(2)}) async-start(f32[8,256,128]{2,1,0:T(8,128)} %broadcast_in_dim.29), calls=%async_computation.2 | async-start | bytes 2097152 | tf_op jit(solution)/shard_map/all_to_all | solution.py:213
  116.0 14.4 %collective-permute-start.10 = (f32[128,256]{1,0:T(8,128)S(1)}, f32[128,256]{1,0:T(8,128)S(1)}, u32[]{:S(2)}, u32[]{:S(2)}) collective-permute-start(f32[128,256]{1,0:T(8,128)S(1)} %get-tuple-element.13), channel_id=1, source_target_pairs={{0,0},{1,16},{2,32},{3,48},{4,64},{5,80},{6,96},{7,112},{8,128},{9... | collective-permute-start | bytes 393224 | tf_op jit(solution)/shard_map/ppermute | solution.py:199
  130.4 16.3 %collective-permute-start.11 = (f32[128,256]{1,0:T(8,128)S(1)}, f32[128,256]{1,0:T(8,128)S(1)}, u32[]{:S(2)}, u32[]{:S(2)}) collective-permute-start(f32[128,256]{1,0:T(8,128)S(1)} %collective-permute-done.10.mine.right), channel_id=1, source_target_pairs={{0,1},{1,0},{2,3},{3,2},{4,5},{5,4},{6,7},{7,6},{8,9},{9,8},{10,11... | collective-permute-start | bytes 393224 | tf_op jit(solution)/shard_map/ppermute | solution.py:200
  138.8 48.1 %collective-permute-start.20 = (f32[8,256,128]{2,1,0:T(8,128)S(1)}, f32[8,256,128]{2,1,0:T(8,128)S(1)}, u32[]{:S(2)}, u32[]{:S(2)}) collective-permute-start(f32[8,256,128]{2,1,0:T(8,128)S(1)} %all-to-all-done.2.mine), channel_id=1, source_target_pairs={{0,16},{16,0},{1,17},{17,1},{2,18},{18,2},{3,19},{19,3},{4,20},{20... | collective-permute-start | bytes 3145736 | tf_op jit(solution)/shard_map/ppermute | solution.py:214
  139.9 13.6 %all-to-all-start.3 = ((f32[16,16,256]{2,1,0:T(8,128)}), f32[16,16,256]{2,1,0:T(8,128)S(1)}, u32[]{:S(2)}, u32[]{:S(2)}) async-start(f32[16,16,256]{2,1,0:T(8,128)} %shard_map.83), calls=%async_computation.3 | async-start | bytes 524288 | tf_op jit(solution)/shard_map/all_to_all | solution.py:206
  146.7 10.9 %collective-permute-start.15 = (f32[2,128,256]{2,1,0:T(8,128)S(1)}, f32[2,128,256]{2,1,0:T(8,128)S(1)}, u32[]{:S(2)}, u32[]{:S(2)}) collective-permute-start(f32[2,128,256]{2,1,0:T(8,128)S(1)} %shard_map.80.refs_0_), channel_id=1, source_target_pairs={{0,14},{2,0},{4,2},{6,4},{8,6},{10,8},{12,10},{14,12},{1,15},{3,1}... | collective-permute-start | bytes 786440 | tf_op jit(solution)/shard_map/ppermute | solution.py:161
  148.5 12.3 %collective-permute-start.12 = (f32[2,128,256]{2,1,0:T(8,128)S(1)}, f32[2,128,256]{2,1,0:T(8,128)S(1)}, u32[]{:S(2)}, u32[]{:S(2)}) collective-permute-start(f32[2,128,256]{2,1,0:T(8,128)S(1)} %shard_map.80.refs_0_), channel_id=1, source_target_pairs={{0,2},{2,4},{4,6},{6,8},{8,10},{10,12},{12,14},{14,0},{1,3},{3,5},... | collective-permute-start | bytes 786440 | tf_op jit(solution)/shard_map/ppermute | solution.py:160
  154.1 13.4 %all-to-all-start.4 = ((f32[8,16,256]{2,1,0:T(8,128)}), f32[8,16,256]{2,1,0:T(8,128)S(1)}, u32[]{:S(2)}, u32[]{:S(2)}) async-start(f32[8,16,256]{2,1,0:T(8,128)} %shard_map.84), calls=%async_computation.4 | async-start | bytes 262144 | tf_op jit(solution)/shard_map/all_to_all | solution.py:207
  157.5 15.5 %copy-start.2 = (f32[2,128,256]{2,1,0:T(8,128)}, f32[2,128,256]{2,1,0:T(8,128)S(1)}, u32[]{:S(2)}) copy-start(f32[2,128,256]{2,1,0:T(8,128)S(1)} %collective-permute-done.15.refs_4_) | copy-start | bytes 786436
  157.5 15.5 %collective-permute-start.16 = (f32[2,128,256]{2,1,0:T(8,128)S(1)}, f32[2,128,256]{2,1,0:T(8,128)}, u32[]{:S(2)}, u32[]{:S(2)}) collective-permute-start(f32[2,128,256]{2,1,0:T(8,128)S(1)} %collective-permute-done.15.refs_4_), channel_id=1, source_target_pairs={{0,14},{2,0},{4,2},{6,4},{8,6},{10,8},{12,10},{14,12},{1,15},{3,1}... | collective-permute-start | bytes 786440 | tf_op jit(solution)/shard_map/ppermute | solution.py:161
  160.8 13.1 %copy-start.4 = (f32[2,128,256]{2,1,0:T(8,128)}, f32[2,128,256]{2,1,0:T(8,128)S(1)}, u32[]{:S(2)}) copy-start(f32[2,128,256]{2,1,0:T(8,128)S(1)} %collective-permute-done.12.refs_1_) | copy-start | bytes 786436
  160.8 13.1 %collective-permute-start.13 = (f32[2,128,256]{2,1,0:T(8,128)S(1)}, f32[2,128,256]{2,1,0:T(8,128)}, u32[]{:S(2)}, u32[]{:S(2)}) collective-permute-start(f32[2,128,256]{2,1,0:T(8,128)S(1)} %collective-permute-done.12.refs_1_), channel_id=1, source_target_pairs={{0,2},{2,4},{4,6},{6,8},{8,10},{10,12},{12,14},{14,0},{1,3},{3,5},... | collective-permute-start | bytes 786440 | tf_op jit(solution)/shard_map/ppermute | solution.py:160
  168.4 16.7 %all-to-all-start.5 = ((f32[32,16,256]{2,1,0:T(8,128)}), f32[32,16,256]{2,1,0:T(8,128)S(1)}, u32[]{:S(2)}, u32[]{:S(2)}) async-start(f32[32,16,256]{2,1,0:T(8,128)} %shard_map.85), calls=%async_computation.5 | async-start | bytes 1048576 | tf_op jit(solution)/shard_map/all_to_all | solution.py:208
  173.1 8.6 %collective-permute-start.17 = (f32[2,128,256]{2,1,0:T(8,128)}, f32[2,128,256]{2,1,0:T(8,128)S(1)}, u32[]{:S(2)}, u32[]{:S(2)}) collective-permute-start(f32[2,128,256]{2,1,0:T(8,128)} %collective-permute-done.16.refs_5_), channel_id=1, source_target_pairs={{0,14},{2,0},{4,2},{6,4},{8,6},{10,8},{12,10},{14,12},{1,15},{3,1}... | collective-permute-start | bytes 786440 | tf_op jit(solution)/shard_map/ppermute | solution.py:161
  173.9 10.4 %collective-permute-start.14 = (f32[2,128,256]{2,1,0:T(8,128)}, f32[2,128,256]{2,1,0:T(8,128)S(1)}, u32[]{:S(2)}, u32[]{:S(2)}) collective-permute-start(f32[2,128,256]{2,1,0:T(8,128)} %collective-permute-done.13.refs_2_), channel_id=1, source_target_pairs={{0,2},{2,4},{4,6},{6,8},{8,10},{10,12},{12,14},{14,0},{1,3},{3,5},... | collective-permute-start | bytes 786440 | tf_op jit(solution)/shard_map/ppermute | solution.py:160
  182.4 6.2 %collective-permute-start.19 = (f32[2,64,256]{2,1,0:T(8,128)}, f32[2,64,256]{2,1,0:T(8,128)S(1)}, u32[]{:S(2)}, u32[]{:S(2)}) collective-permute-start(f32[2,64,256]{2,1,0:T(8,128)} %slice.19), channel_id=1, source_target_pairs={{0,14},{2,0},{4,2},{6,4},{8,6},{10,8},{12,10},{14,12},{1,15},{3,1}... | collective-permute-start | bytes 393224 | tf_op jit(solution)/shard_map/ppermute | solution.py:163
  185.0 6.5 %collective-permute-start.18 = (f32[2,64,256]{2,1,0:T(8,128)}, f32[2,64,256]{2,1,0:T(8,128)}, u32[]{:S(2)}, u32[]{:S(2)}) collective-permute-start(f32[2,64,256]{2,1,0:T(8,128)} %slice.18), channel_id=1, source_target_pairs={{0,2},{2,4},{4,6},{6,8},{8,10},{10,12},{12,14},{14,0},{1,3},{3,5},... | collective-permute-start | bytes 393224 | tf_op jit(solution)/shard_map/ppermute | solution.py:162
  185.1 1.0 copy-start.1
  186.1 5.3 %copy-start.3 = (f32[2,128,256]{2,1,0:T(8,128)S(1)}, f32[2,128,256]{2,1,0:T(8,128)}, u32[]{:S(2)}) copy-start(f32[2,128,256]{2,1,0:T(8,128)} %copy-done.2) | copy-start | bytes 786436
  186.1 5.3 %copy-start.5 = (f32[2,128,256]{2,1,0:T(8,128)S(1)}, f32[2,128,256]{2,1,0:T(8,128)}, u32[]{:S(2)}) copy-start(f32[2,128,256]{2,1,0:T(8,128)} %copy-done.4) | copy-start | bytes 786436

commit v2 on v1

--- a/solution.py
+++ b/solution.py
@@ -83,6 +83,24 @@
     return call(second_kernel, [out], [SMEM, block, block, whole], [out_block], **rest)(number, *left, right)
 
 
+def last_kernel(at, high, low, top, bottom, term, *rest):
+    *more, out = rest
+    depth = pl.ds(pl.multiple_of(at[0] * 128, 128), 128)
+    columns = pl.ds(pl.multiple_of(at[1] * 256, 256), 256)
+    right = halves(jnp.concatenate([top[:, columns], bottom[:, columns]]))
+    for k in range(4):
+        rows = slice(k * 256, k * 256 + 256)
+        total = term[rows] + dot3((high[rows, depth], low[rows, depth]), right)
+        out[rows] = total + more[0][rows] if more else total
+
+
+def add_last(at, kept, top, bottom, *terms):
+    out = ((1024, 256), jnp.float32)
+    return call(last_kernel, [out], [SMEM] + [VMEM] * (4 + len(terms)), [VMEM], flops=3 << 26)(
+        at, *kept, top, bottom, *terms
+    )
+
+
 def chunk_kernel(slots, at, pattern, dealt, out):
     for number in range(2):
         mask = pattern[number, at[0]].astype(jnp.float32)
@@ -186,11 +204,14 @@
         owner_slot, (row * 4 + col // 4)[None], pattern, dealt
     )
     block = both(chunk, lax.ppermute(chunk, "xh", SWAP), xh == 0).reshape(128, 512)
-    masked = gather_rows(ring(block), z)
+    *came, top, bottom = ring(block)
+    masked = gather_rows(came, z)
 
     sent, *kept = product((1 - core)[None], [inverse_rows], masked)
+    term = product(core[None], kept, masked)
+    sent = add_last(jnp.stack([(z + 4) % 8, 1 - core]), kept, top, bottom, sent)
     received = lax.ppermute(sent, "core", SWAP)
-    term = product(core[None], kept, masked) + received
+    term = add_last(jnp.stack([(z + 4) % 8, core]), kept, top, bottom, term, received)
     terms = lax.all_to_all(term.reshape(8, 128, 256), CHIP, 0, 0, tiled=True)
     outs = [((128, 256), jnp.float32), ((256, 128), jnp.float32)]
     at = jnp.stack([core, col * 4 + chip // 2])

time: 195 us -> 194 us (level)
  Pallas kernels: 14.1 us -> 17.3 us
  waiting for transfers between devices: 116 us -> 113 us
    pallas_call x0 -> x2, Pallas kernels: none -> 3.2 us  [add_last(): call(last_kernel, [out], [SMEM] + [VMEM] * (4 + len(terms)), [VMEM], flop...]
    ppermute x2, waiting for transfers between devices: 8.91 us -> 6.07 us  [ring(): top = lax.ppermute(ups[-1][..., :half, :], 'z', UP)]
  transfers between devices with their start and end apart: 27 -> 27, of which waited for: 14 -> 13; matrix products, arithmetic and copies ran while one was open for 1% -> 1% of each run, Pallas kernels for 4% -> 5%
where the time goes in v2:
time: 194 us
  waiting for transfers between devices  113 us (58%)
  starting transfers between devices  58.1 us (30%)
  Pallas kernels  17.3 us (9%)
  local copies, waits for them, and re-layouts  3.88 us (2%)
    all_to_all x1, waiting for transfers between devices, shards(): lax.all_to_all(panels[0].reshape(16, 64, 256), COL, 0, 0, tiled=True)  30.1 us
    ppermute x6, waiting for transfers between devices, ring(): downs.append(lax.ppermute(downs[-1], 'z', DOWN))  23.5 us
    all_to_all x1, waiting for transfers between devices, shards(): terms = lax.all_to_all(term.reshape(8, 128, 256), CHIP, 0, 0, tiled=True)  15.1 us
    ppermute x1, waiting for transfers between devices, shards(): mine = lax.ppermute(column, ALL, TRANSPOSE)  12.4 us
    all_to_all x1, starting transfers between devices, shards(): lax.all_to_all(panels[0].reshape(16, 64, 256), COL, 0, 0, tiled=True)  10.3 us
    all_to_all x1, waiting for transfers between devices, shards(): turned = lax.all_to_all(turned, CHIP, 0, 0, tiled=True)  8.59 us
    ppermute x6, starting transfers between devices, ring(): downs.append(lax.ppermute(downs[-1], 'z', DOWN))  7.6 us
    all_to_all x1, starting transfers between devices, shards(): inner = add_up(lax.all_to_all(inner, ROW, 0, 0, tiled=True), 8)  6.92 us
  transfers between devices with their start and end apart: 27, of which 13 were waited for; matrix products, arithmetic and copies ran while one was open for 1% of the time, Pallas kernels for 5%

profile of v2, /device:TPU:2, one launch (start us, length us, event | category | flops | bytes accessed | tf_op | source)
XLA Modules:
  0.0 193.6 jit_solution(10855129839884269499)
XLA Ops:
  0.7 10.3 %all-to-all-start = ((f32[16,64,256]{2,1,0:T(8,128)}), f32[16,64,256]{2,1,0:T(8,128)S(1)}, u32[]{:S(2)}, u32[]{:S(2)}) async-start(f32[16,64,256]{2,1,0:T(8,128)} %bitcast.17), calls=%async_computation | async-start | bytes 2097152 | tf_op jit(solution)/shard_map/all_to_all | solution.py:201
  11.0 30.1 %all-to-all-done.dealt = f32[16,64,256]{2,1,0:T(8,128)S(1)} async-done(((f32[16,64,256]{2,1,0:T(8,128)}), f32[16,64,256]{2,1,0:T(8,128)S(1)}, u32[]{:S(2)}, u32[]{:S(2)}) %all-to-all-start) | async-done | bytes 1048608 | tf_op jit(solution)/shard_map/all_to_all | solution.py:201
  41.1 0.6 shard_map.76
  41.7 0.5 collective-permute-start
  42.2 6.0 %collective-permute-done = f32[64,512]{1,0:T(8,128)S(1)} collective-permute-done((f32[64,512]{1,0:T(8,128)S(1)}, f32[64,512]{1,0:T(8,128)S(1)}, u32[]{:S(2)}, u32[]{:S(2)}) %collective-permute-start) | collective-permute-done | bytes 131104 | tf_op jit(solution)/shard_map/ppermute | solution.py:206
  48.4 2.0 %collective-permute-start.1 = (f32[128,512]{1,0:T(8,128)S(1)}, f32[128,512]{1,0:T(8,128)S(1)}, u32[]{:S(2)}, u32[]{:S(2)}) collective-permute-start(f32[128,512]{1,0:T(8,128)S(1)} %bitcast.13), channel_id=1, source_target_pairs={{0,2},{2,4},{4,6},{6,8},{8,10},{10,12},{12,14},{14,0},{1,3},{3,5},... | collective-permute-start | bytes 786440 | tf_op jit(solution)/shard_map/ppermute | solution.py:178
  50.4 6.9 %collective-permute-done.4 = f32[128,512]{1,0:T(8,128)S(1)} collective-permute-done((f32[128,512]{1,0:T(8,128)S(1)}, f32[128,512]{1,0:T(8,128)S(1)}, u32[]{:S(2)}, u32[]{:S(2)}) %collective-permute-start.4) | collective-permute-done | bytes 262176 | tf_op jit(solution)/shard_map/ppermute | solution.py:179
  57.3 2.2 %collective-permute-start.2 = (f32[128,512]{1,0:T(8,128)S(1)}, f32[128,512]{1,0:T(8,128)S(1)}, u32[]{:S(2)}, u32[]{:S(2)}) collective-permute-start(f32[128,512]{1,0:T(8,128)S(1)} %collective-permute-done.1), channel_id=1, source_target_pairs={{0,2},{2,4},{4,6},{6,8},{8,10},{10,12},{12,14},{14,0},{1,3},{3,5},... | collective-permute-start | bytes 786440 | tf_op jit(solution)/shard_map/ppermute | solution.py:178
  59.6 6.1 %collective-permute-done.5 = f32[128,512]{1,0:T(8,128)S(1)} collective-permute-done((f32[128,512]{1,0:T(8,128)S(1)}, f32[128,512]{1,0:T(8,128)S(1)}, u32[]{:S(2)}, u32[]{:S(2)}) %collective-permute-start.5) | collective-permute-done | bytes 262176 | tf_op jit(solution)/shard_map/ppermute | solution.py:179
  65.7 1.6 collective-permute-start.6
  67.4 0.4 collective-permute-start.3
  68.2 3.9 %collective-permute-done.6 = f32[128,512]{1,0:T(8,128)S(1)} collective-permute-done((f32[128,512]{1,0:T(8,128)S(1)}, f32[128,512]{1,0:T(8,128)S(1)}, u32[]{:S(2)}, u32[]{:S(2)}) %collective-permute-start.6) | collective-permute-done | bytes 262176 | tf_op jit(solution)/shard_map/ppermute | solution.py:179
  72.1 3.6 %collective-permute-start.8 = (f32[64,512]{1,0:T(8,128)S(1)}, f32[64,512]{1,0:T(8,128)S(1)}, u32[]{:S(2)}, u32[]{:S(2)}) collective-permute-start(f32[64,512]{1,0:T(8,128)S(1)} %slice.17), channel_id=1, source_target_pairs={{0,14},{2,0},{4,2},{6,4},{8,6},{10,8},{12,10},{14,12},{1,15},{3,1}... | collective-permute-start | bytes 393224 | tf_op jit(solution)/shard_map/ppermute | solution.py:181
  76.0 2.7 %shard_map.77 = (f32[1024,256]{1,0:T(8,128)S(1)}, bf16[1024,1024]{1,0:T(8,128)(2,1)S(1)}, bf16[1024,1024]{1,0:T(8,128)(2,1)S(1)}) custom-call(s32[1]{0:T(128)} %bitcast.5.number, f32[1024,1024]{1,0:T(8,128)S(1)} %copy-done, f32[1024,512]{1,0:T(8,128)S(1)} %constant_dynamic-update-slice_fusion.right), custom_call_target="tpu_custom_call" | custom-call | flops 1610612736 | bytes 7340032 | tf_op jit(solution)/shard_map/pallas_call | solution.py:82
  78.7 3.3 %collective-permute-done.7.top = f32[64,512]{1,0:T(8,128)S(1)} collective-permute-done((f32[64,512]{1,0:T(8,128)S(1)}, f32[64,512]{1,0:T(8,128)S(1)}, u32[]{:S(2)}, u32[]{:S(2)}) %collective-permute-start.7) | collective-permute-done | bytes 131104 | tf_op jit(solution)/shard_map/ppermute | solution.py:180
  82.0 1.1 shard_map.79
  83.3 2.6 %shard_map.78.term = f32[1024,256]{1,0:T(8,128)S(1)} custom-call(s32[1]{0:T(128)} %bitcast.2.number.core, bf16[1024,1024]{1,0:T(8,128)(2,1)S(1)} %get-tuple-element.10.high, bf16[1024,1024]{1,0:T(8,128)(2,1)S(1)} %get-tuple-element.11.low, f32[1024,512]{1,0:T(8,128)S(1)} %constant_dynamic-update-slice_fusion.right), custom_call_target="tpu_custom_call" | custom-call | flops 1610612736 | bytes 7340032 | tf_op jit(solution)/shard_map/pallas_call | solution.py:83
  85.9 2.1 %shard_map.80 = f32[1024,256]{1,0:T(8,128)} custom-call(s32[2]{0:T(128)S(1)} %pad_add_fusion.1.at, bf16[1024,1024]{1,0:T(8,128)(2,1)S(1)} %get-tuple-element.10.high, bf16[1024,1024]{1,0:T(8,128)(2,1)S(1)} %get-tuple-element.11.low, f32[64,512]{1,0:T(8,128)S(1)} %collective-permute-done.7.top, f32[64,512]{1,0:T(8,128)S(1)} %collective-permute-done.8.bottom, ...), custom_call_target="tpu_custom_call" | custom-call | flops 201326592 | bytes 2097152 | tf_op jit(solution)/shard_map/pallas_call | solution.py:99
  87.9 5.9 %all-to-all-start.1 = ((f32[8,128,256]{2,1,0:T(8,128)}), f32[8,128,256]{2,1,0:T(8,128)S(1)}, u32[]{:S(2)}, u32[]{:S(2)}) async-start(f32[8,128,256]{2,1,0:T(8,128)} %bitcast.11), calls=%async_computation.1 | async-start | bytes 2097152 | tf_op jit(solution)/shard_map/all_to_all | solution.py:215
  94.0 15.1 %all-to-all-done.1.terms = f32[8,128,256]{2,1,0:T(8,128)S(1)} async-done(((f32[8,128,256]{2,1,0:T(8,128)}), f32[8,128,256]{2,1,0:T(8,128)S(1)}, u32[]{:S(2)}, u32[]{:S(2)}) %all-to-all-start.1) | async-done | bytes 1048608 | tf_op jit(solution)/shard_map/all_to_all | solution.py:215
  109.1 0.7 shard_map.81
  109.7 1.0 broadcast_in_dim.29
  110.8 4.7 %all-to-all-start.2 = ((f32[8,256,128]{2,1,0:T(8,128)}), f32[8,256,128]{2,1,0:T(8,128)S(1)}, u32[]{:S(2)}, u32[]{:S(2)}) async-start(f32[8,256,128]{2,1,0:T(8,128)} %broadcast_in_dim.29), calls=%async_computation.2 | async-start | bytes 2097152 | tf_op jit(solution)/shard_map/all_to_all | solution.py:234
  115.5 1.9 collective-permute-start.10
  117.4 12.4 %collective-permute-done.10.mine.right = f32[128,256]{1,0:T(8,128)S(1)} collective-permute-done((f32[128,256]{1,0:T(8,128)S(1)}, f32[128,256]{1,0:T(8,128)S(1)}, u32[]{:S(2)}, u32[]{:S(2)}) %collective-permute-start.10) | collective-permute-done | bytes 131104 | tf_op jit(solution)/shard_map/ppermute | solution.py:220
  129.8 8.6 %all-to-all-done.2.mine = f32[8,256,128]{2,1,0:T(8,128)S(1)} async-done(((f32[8,256,128]{2,1,0:T(8,128)}), f32[8,256,128]{2,1,0:T(8,128)S(1)}, u32[]{:S(2)}, u32[]{:S(2)}) %all-to-all-start.2) | async-done | bytes 1048608 | tf_op jit(solution)/shard_map/all_to_all | solution.py:234
  138.4 1.0 shard_map.85
  139.4 6.9 %all-to-all-start.3 = ((f32[16,16,256]{2,1,0:T(8,128)}), f32[16,16,256]{2,1,0:T(8,128)S(1)}, u32[]{:S(2)}, u32[]{:S(2)}) async-start(f32[16,16,256]{2,1,0:T(8,128)} %shard_map.85), calls=%async_computation.3 | async-start | bytes 524288 | tf_op jit(solution)/shard_map/all_to_all | solution.py:227
  146.4 1.9 %collective-permute-start.15 = (f32[2,128,256]{2,1,0:T(8,128)S(1)}, f32[2,128,256]{2,1,0:T(8,128)S(1)}, u32[]{:S(2)}, u32[]{:S(2)}) collective-permute-start(f32[2,128,256]{2,1,0:T(8,128)S(1)} %shard_map.82.refs_0_), channel_id=1, source_target_pairs={{0,14},{2,0},{4,2},{6,4},{8,6},{10,8},{12,10},{14,12},{1,15},{3,1}... | collective-permute-start | bytes 786440 | tf_op jit(solution)/shard_map/ppermute | solution.py:179
  148.3 0.3 collective-permute-start.12
  148.7 4.5 %all-to-all-done.3.pieces = f32[16,16,256]{2,1,0:T(8,128)S(1)} async-done(((f32[16,16,256]{2,1,0:T(8,128)}), f32[16,16,256]{2,1,0:T(8,128)S(1)}, u32[]{:S(2)}, u32[]{:S(2)}) %all-to-all-start.3) | async-done | bytes 262176 | tf_op jit(solution)/shard_map/all_to_all | solution.py:227
  153.2 0.7 shard_map.86
  153.8 3.4 %all-to-all-start.4 = ((f32[8,16,256]{2,1,0:T(8,128)}), f32[8,16,256]{2,1,0:T(8,128)S(1)}, u32[]{:S(2)}, u32[]{:S(2)}) async-start(f32[8,16,256]{2,1,0:T(8,128)} %shard_map.86), calls=%async_computation.4 | async-start | bytes 262144 | tf_op jit(solution)/shard_map/all_to_all | solution.py:228
  157.2 3.2 %collective-permute-start.16 = (f32[2,128,256]{2,1,0:T(8,128)S(1)}, f32[2,128,256]{2,1,0:T(8,128)}, u32[]{:S(2)}, u32[]{:S(2)}) collective-permute-start(f32[2,128,256]{2,1,0:T(8,128)S(1)} %collective-permute-done.15.refs_4_), channel_id=1, source_target_pairs={{0,14},{2,0},{4,2},{6,4},{8,6},{10,8},{12,10},{14,12},{1,15},{3,1}... | collective-permute-start | bytes 786440 | tf_op jit(solution)/shard_map/ppermute | solution.py:179
  160.5 6.7 %all-to-all-done.4.pieces = f32[8,16,256]{2,1,0:T(8,128)S(1)} async-done(((f32[8,16,256]{2,1,0:T(8,128)}), f32[8,16,256]{2,1,0:T(8,128)S(1)}, u32[]{:S(2)}, u32[]{:S(2)}) %all-to-all-start.4) | async-done | bytes 131104 | tf_op jit(solution)/shard_map/all_to_all | solution.py:228
  167.2 0.9 shard_map.87
  168.1 4.7 %all-to-all-start.5 = ((f32[32,16,256]{2,1,0:T(8,128)}), f32[32,16,256]{2,1,0:T(8,128)S(1)}, u32[]{:S(2)}, u32[]{:S(2)}) async-start(f32[32,16,256]{2,1,0:T(8,128)} %shard_map.87), calls=%async_computation.5 | async-start | bytes 1048576 | tf_op jit(solution)/shard_map/all_to_all | solution.py:229
  172.8 0.7 collective-permute-start.17
  173.5 1.4 collective-permute-start.14
  174.9 6.5 %collective-permute-done.17.refs_6_ = f32[2,128,256]{2,1,0:T(8,128)S(1)} collective-permute-done((f32[2,128,256]{2,1,0:T(8,128)}, f32[2,128,256]{2,1,0:T(8,128)S(1)}, u32[]{:S(2)}, u32[]{:S(2)}) %collective-permute-start.17) | collective-permute-done | bytes 262176 | tf_op jit(solution)/shard_map/ppermute | solution.py:179
  181.4 0.7 slice.19
  182.1 1.8 collective-permute-start.19
  183.9 0.7 slice.18
  184.8 1.0 copy-done.1
  185.8 0.8 shard_map.88
  186.7 1.6 shard_map.83
  188.3 2.8 %collective-permute-done.18.refs_7_ = f32[2,64,256]{2,1,0:T(8,128)} collective-permute-done((f32[2,64,256]{2,1,0:T(8,128)}, f32[2,64,256]{2,1,0:T(8,128)}, u32[]{:S(2)}, u32[]{:S(2)}) %collective-permute-start.18) | collective-permute-done | bytes 131104 | tf_op jit(solution)/shard_map/ppermute | solution.py:180
  191.1 2.5 %shard_map.84 = f32[2,1024,256]{2,1,0:T(8,128)} custom-call(s32[1]{0:T(128)} %bitcast.z, f32[2,128,256]{2,1,0:T(8,128)S(1)} %shard_map.82.refs_0_, f32[2,128,256]{2,1,0:T(8,128)S(1)} %copy-done.5, f32[2,128,256]{2,1,0:T(8,128)} %collective-permute-done.13.refs_2_, f32[2,128,256]{2,1,0:T(8,128)S(1)} %collective-permute-done.14.refs_3_, ...), custom_call_target="tpu_custom_call" | custom-call | bytes 4194304 | tf_op jit(solution)/shard_map/pallas_call | solution.py:240
  (52 shorter events, 1.2 us)
Async XLA Ops:
  0.6 40.5 %copy-start.6 = (s32[2,64]{1,0:T(2,128)S(1)}, s32[2,64]{1,0:T(2,128)}, u32[]{:S(2)}) copy-start(s32[2,64]{1,0:T(2,128)} %pattern.3) | copy-start | bytes 1540
  0.6 40.5 %copy-start.7 = (s32[2]{0:T(128)S(1)}, s32[2]{0:T(128)}, u32[]{:S(2)}) copy-start(s32[2]{0:T(128)} %slots.1) | copy-start | bytes 28
  0.7 40.5 %all-to-all-start = ((f32[16,64,256]{2,1,0:T(8,128)}), f32[16,64,256]{2,1,0:T(8,128)S(1)}, u32[]{:S(2)}, u32[]{:S(2)}) async-start(f32[16,64,256]{2,1,0:T(8,128)} %bitcast.17), calls=%async_computation | async-start | bytes 2097152 | tf_op jit(solution)/shard_map/all_to_all | solution.py:201
  41.7 6.6 %collective-permute-start = (f32[64,512]{1,0:T(8,128)S(1)}, f32[64,512]{1,0:T(8,128)S(1)}, u32[]{:S(2)}, u32[]{:S(2)}) collective-permute-start(f32[64,512]{1,0:T(8,128)S(1)} %shard_map.76), channel_id=1, source_target_pairs={{0,1},{1,0},{2,3},{3,2},{4,5},{5,4},{6,7},{7,6},{8,9},{9,8},{10,11... | collective-permute-start | bytes 393224 | tf_op jit(solution)/shard_map/ppermute | solution.py:206
  48.3 9.0 %collective-permute-start.4 = (f32[128,512]{1,0:T(8,128)S(1)}, f32[128,512]{1,0:T(8,128)S(1)}, u32[]{:S(2)}, u32[]{:S(2)}) collective-permute-start(f32[128,512]{1,0:T(8,128)S(1)} %bitcast.12), channel_id=1, source_target_pairs={{0,14},{2,0},{4,2},{6,4},{8,6},{10,8},{12,10},{14,12},{1,15},{3,1}... | collective-permute-start | bytes 786440 | tf_op jit(solution)/shard_map/ppermute | solution.py:179
  48.4 8.9 %collective-permute-start.1 = (f32[128,512]{1,0:T(8,128)S(1)}, f32[128,512]{1,0:T(8,128)S(1)}, u32[]{:S(2)}, u32[]{:S(2)}) collective-permute-start(f32[128,512]{1,0:T(8,128)S(1)} %bitcast.13), channel_id=1, source_target_pairs={{0,2},{2,4},{4,6},{6,8},{8,10},{10,12},{12,14},{14,0},{1,3},{3,5},... | collective-permute-start | bytes 786440 | tf_op jit(solution)/shard_map/ppermute | solution.py:178
  57.3 8.5 %collective-permute-start.5 = (f32[128,512]{1,0:T(8,128)S(1)}, f32[128,512]{1,0:T(8,128)S(1)}, u32[]{:S(2)}, u32[]{:S(2)}) collective-permute-start(f32[128,512]{1,0:T(8,128)S(1)} %collective-permute-done.4), channel_id=1, source_target_pairs={{0,14},{2,0},{4,2},{6,4},{8,6},{10,8},{12,10},{14,12},{1,15},{3,1}... | collective-permute-start | bytes 786440 | tf_op jit(solution)/shard_map/ppermute | solution.py:179
  57.3 10.1 %collective-permute-start.2 = (f32[128,512]{1,0:T(8,128)S(1)}, f32[128,512]{1,0:T(8,128)S(1)}, u32[]{:S(2)}, u32[]{:S(2)}) collective-permute-start(f32[128,512]{1,0:T(8,128)S(1)} %collective-permute-done.1), channel_id=1, source_target_pairs={{0,2},{2,4},{4,6},{6,8},{8,10},{10,12},{12,14},{14,0},{1,3},{3,5},... | collective-permute-start | bytes 786440 | tf_op jit(solution)/shard_map/ppermute | solution.py:178
  65.7 6.4 %collective-permute-start.6 = (f32[128,512]{1,0:T(8,128)S(1)}, f32[128,512]{1,0:T(8,128)S(1)}, u32[]{:S(2)}, u32[]{:S(2)}) collective-permute-start(f32[128,512]{1,0:T(8,128)S(1)} %collective-permute-done.5), channel_id=1, source_target_pairs={{0,14},{2,0},{4,2},{6,4},{8,6},{10,8},{12,10},{14,12},{1,15},{3,1}... | collective-permute-start | bytes 786440 | tf_op jit(solution)/shard_map/ppermute | solution.py:179
  67.4 8.3 %collective-permute-start.3 = (f32[128,512]{1,0:T(8,128)S(1)}, f32[128,512]{1,0:T(8,128)S(1)}, u32[]{:S(2)}, u32[]{:S(2)}) collective-permute-start(f32[128,512]{1,0:T(8,128)S(1)} %collective-permute-done.2), channel_id=1, source_target_pairs={{0,2},{2,4},{4,6},{6,8},{8,10},{10,12},{12,14},{14,0},{1,3},{3,5},... | collective-permute-start | bytes 786440 | tf_op jit(solution)/shard_map/ppermute | solution.py:178
  68.1 7.9 %copy-start = (f32[1024,1024]{1,0:T(8,128)S(1)}, f32[1024,1024]{1,0:T(8,128)}, u32[]{:S(2)}) copy-start(f32[1024,1024]{1,0:T(8,128)} %left.1) | copy-start | bytes 12582916
  72.1 6.6 %collective-permute-start.8 = (f32[64,512]{1,0:T(8,128)S(1)}, f32[64,512]{1,0:T(8,128)S(1)}, u32[]{:S(2)}, u32[]{:S(2)}) collective-permute-start(f32[64,512]{1,0:T(8,128)S(1)} %slice.17), channel_id=1, source_target_pairs={{0,14},{2,0},{4,2},{6,4},{8,6},{10,8},{12,10},{14,12},{1,15},{3,1}... | collective-permute-start | bytes 393224 | tf_op jit(solution)/shard_map/ppermute | solution.py:181
  75.7 6.3 %collective-permute-start.7 = (f32[64,512]{1,0:T(8,128)S(1)}, f32[64,512]{1,0:T(8,128)S(1)}, u32[]{:S(2)}, u32[]{:S(2)}) collective-permute-start(f32[64,512]{1,0:T(8,128)S(1)} %slice.16), channel_id=1, source_target_pairs={{0,2},{2,4},{4,6},{6,8},{8,10},{10,12},{12,14},{14,0},{1,3},{3,5},... | collective-permute-start | bytes 393224 | tf_op jit(solution)/shard_map/ppermute | solution.py:180
  83.1 2.8 %collective-permute-start.9 = (f32[1024,256]{1,0:T(8,128)S(1)}, f32[1024,256]{1,0:T(8,128)S(1)}, u32[]{:S(2)}, u32[]{:S(2)}) collective-permute-start(f32[1024,256]{1,0:T(8,128)S(1)} %shard_map.79), channel_id=1, source_target_pairs={{0,16},{16,0},{1,17},{17,1},{2,18},{18,2},{3,19},{19,3},{4,20},{20... | collective-permute-start | bytes 3145736 | tf_op jit(solution)/shard_map/ppermute | solution.py:213
  87.9 21.1 %all-to-all-start.1 = ((f32[8,128,256]{2,1,0:T(8,128)}), f32[8,128,256]{2,1,0:T(8,128)S(1)}, u32[]{:S(2)}, u32[]{:S(2)}) async-start(f32[8,128,256]{2,1,0:T(8,128)} %bitcast.11), calls=%async_computation.1 | async-start | bytes 2097152 | tf_op jit(solution)/shard_map/all_to_all | solution.py:215
  110.8 27.6 %all-to-all-start.2 = ((f32[8,256,128]{2,1,0:T(8,128)}), f32[8,256,128]{2,1,0:T(8,128)S(1)}, u32[]{:S(2)}, u32[]{:S(2)}) async-start(f32[8,256,128]{2,1,0:T(8,128)} %broadcast_in_dim.29), calls=%async_computation.2 | async-start | bytes 2097152 | tf_op jit(solution)/shard_map/all_to_all | solution.py:234
  115.5 14.3 %collective-permute-start.10 = (f32[128,256]{1,0:T(8,128)S(1)}, f32[128,256]{1,0:T(8,128)S(1)}, u32[]{:S(2)}, u32[]{:S(2)}) collective-permute-start(f32[128,256]{1,0:T(8,128)S(1)} %get-tuple-element.13), channel_id=1, source_target_pairs={{0,0},{1,16},{2,32},{3,48},{4,64},{5,80},{6,96},{7,112},{8,128},{9... | collective-permute-start | bytes 393224 | tf_op jit(solution)/shard_map/ppermute | solution.py:220
  129.8 16.5 %collective-permute-start.11 = (f32[128,256]{1,0:T(8,128)S(1)}, f32[128,256]{1,0:T(8,128)S(1)}, u32[]{:S(2)}, u32[]{:S(2)}) collective-permute-start(f32[128,256]{1,0:T(8,128)S(1)} %collective-permute-done.10.mine.right), channel_id=1, source_target_pairs={{0,1},{1,0},{2,3},{3,2},{4,5},{5,4},{6,7},{7,6},{8,9},{9,8},{10,11... | collective-permute-start | bytes 393224 | tf_op jit(solution)/shard_map/ppermute | solution.py:221
  138.4 48.3 %collective-permute-start.20 = (f32[8,256,128]{2,1,0:T(8,128)S(1)}, f32[8,256,128]{2,1,0:T(8,128)S(1)}, u32[]{:S(2)}, u32[]{:S(2)}) collective-permute-start(f32[8,256,128]{2,1,0:T(8,128)S(1)} %all-to-all-done.2.mine), channel_id=1, source_target_pairs={{0,16},{16,0},{1,17},{17,1},{2,18},{18,2},{3,19},{19,3},{4,20},{20... | collective-permute-start | bytes 3145736 | tf_op jit(solution)/shard_map/ppermute | solution.py:235
  139.4 13.7 %all-to-all-start.3 = ((f32[16,16,256]{2,1,0:T(8,128)}), f32[16,16,256]{2,1,0:T(8,128)S(1)}, u32[]{:S(2)}, u32[]{:S(2)}) async-start(f32[16,16,256]{2,1,0:T(8,128)} %shard_map.85), calls=%async_computation.3 | async-start | bytes 524288 | tf_op jit(solution)/shard_map/all_to_all | solution.py:227
  146.4 10.9 %collective-permute-start.15 = (f32[2,128,256]{2,1,0:T(8,128)S(1)}, f32[2,128,256]{2,1,0:T(8,128)S(1)}, u32[]{:S(2)}, u32[]{:S(2)}) collective-permute-start(f32[2,128,256]{2,1,0:T(8,128)S(1)} %shard_map.82.refs_0_), channel_id=1, source_target_pairs={{0,14},{2,0},{4,2},{6,4},{8,6},{10,8},{12,10},{14,12},{1,15},{3,1}... | collective-permute-start | bytes 786440 | tf_op jit(solution)/shard_map/ppermute | solution.py:179
  148.3 12.2 %collective-permute-start.12 = (f32[2,128,256]{2,1,0:T(8,128)S(1)}, f32[2,128,256]{2,1,0:T(8,128)S(1)}, u32[]{:S(2)}, u32[]{:S(2)}) collective-permute-start(f32[2,128,256]{2,1,0:T(8,128)S(1)} %shard_map.82.refs_0_), channel_id=1, source_target_pairs={{0,2},{2,4},{4,6},{6,8},{8,10},{10,12},{12,14},{14,0},{1,3},{3,5},... | collective-permute-start | bytes 786440 | tf_op jit(solution)/shard_map/ppermute | solution.py:178
  153.8 13.4 %all-to-all-start.4 = ((f32[8,16,256]{2,1,0:T(8,128)}), f32[8,16,256]{2,1,0:T(8,128)S(1)}, u32[]{:S(2)}, u32[]{:S(2)}) async-start(f32[8,16,256]{2,1,0:T(8,128)} %shard_map.86), calls=%async_computation.4 | async-start | bytes 262144 | tf_op jit(solution)/shard_map/all_to_all | solution.py:228
  157.2 15.5 %copy-start.2 = (f32[2,128,256]{2,1,0:T(8,128)}, f32[2,128,256]{2,1,0:T(8,128)S(1)}, u32[]{:S(2)}) copy-start(f32[2,128,256]{2,1,0:T(8,128)S(1)} %collective-permute-done.15.refs_4_) | copy-start | bytes 786436
  157.2 15.5 %collective-permute-start.16 = (f32[2,128,256]{2,1,0:T(8,128)S(1)}, f32[2,128,256]{2,1,0:T(8,128)}, u32[]{:S(2)}, u32[]{:S(2)}) collective-permute-start(f32[2,128,256]{2,1,0:T(8,128)S(1)} %collective-permute-done.15.refs_4_), channel_id=1, source_target_pairs={{0,14},{2,0},{4,2},{6,4},{8,6},{10,8},{12,10},{14,12},{1,15},{3,1}... | collective-permute-start | bytes 786440 | tf_op jit(solution)/shard_map/ppermute | solution.py:179
  160.5 13.0 %copy-start.4 = (f32[2,128,256]{2,1,0:T(8,128)}, f32[2,128,256]{2,1,0:T(8,128)S(1)}, u32[]{:S(2)}) copy-start(f32[2,128,256]{2,1,0:T(8,128)S(1)} %collective-permute-done.12.refs_1_) | copy-start | bytes 786436
  160.5 13.0 %collective-permute-start.13 = (f32[2,128,256]{2,1,0:T(8,128)S(1)}, f32[2,128,256]{2,1,0:T(8,128)}, u32[]{:S(2)}, u32[]{:S(2)}) collective-permute-start(f32[2,128,256]{2,1,0:T(8,128)S(1)} %collective-permute-done.12.refs_1_), channel_id=1, source_target_pairs={{0,2},{2,4},{4,6},{6,8},{8,10},{10,12},{12,14},{14,0},{1,3},{3,5},... | collective-permute-start | bytes 786440 | tf_op jit(solution)/shard_map/ppermute | solution.py:178
  168.1 16.7 %all-to-all-start.5 = ((f32[32,16,256]{2,1,0:T(8,128)}), f32[32,16,256]{2,1,0:T(8,128)S(1)}, u32[]{:S(2)}, u32[]{:S(2)}) async-start(f32[32,16,256]{2,1,0:T(8,128)} %shard_map.87), calls=%async_computation.5 | async-start | bytes 1048576 | tf_op jit(solution)/shard_map/all_to_all | solution.py:229
  172.8 8.6 %collective-permute-start.17 = (f32[2,128,256]{2,1,0:T(8,128)}, f32[2,128,256]{2,1,0:T(8,128)S(1)}, u32[]{:S(2)}, u32[]{:S(2)}) collective-permute-start(f32[2,128,256]{2,1,0:T(8,128)} %collective-permute-done.16.refs_5_), channel_id=1, source_target_pairs={{0,14},{2,0},{4,2},{6,4},{8,6},{10,8},{12,10},{14,12},{1,15},{3,1}... | collective-permute-start | bytes 786440 | tf_op jit(solution)/shard_map/ppermute | solution.py:179
  173.5 10.4 %collective-permute-start.14 = (f32[2,128,256]{2,1,0:T(8,128)}, f32[2,128,256]{2,1,0:T(8,128)S(1)}, u32[]{:S(2)}, u32[]{:S(2)}) collective-permute-start(f32[2,128,256]{2,1,0:T(8,128)} %collective-permute-done.13.refs_2_), channel_id=1, source_target_pairs={{0,2},{2,4},{4,6},{6,8},{8,10},{10,12},{12,14},{14,0},{1,3},{3,5},... | collective-permute-start | bytes 786440 | tf_op jit(solution)/shard_map/ppermute | solution.py:178
  182.1 6.2 %collective-permute-start.19 = (f32[2,64,256]{2,1,0:T(8,128)}, f32[2,64,256]{2,1,0:T(8,128)S(1)}, u32[]{:S(2)}, u32[]{:S(2)}) collective-permute-start(f32[2,64,256]{2,1,0:T(8,128)} %slice.19), channel_id=1, source_target_pairs={{0,14},{2,0},{4,2},{6,4},{8,6},{10,8},{12,10},{14,12},{1,15},{3,1}... | collective-permute-start | bytes 393224 | tf_op jit(solution)/shard_map/ppermute | solution.py:181
  184.6 6.5 %collective-permute-start.18 = (f32[2,64,256]{2,1,0:T(8,128)}, f32[2,64,256]{2,1,0:T(8,128)}, u32[]{:S(2)}, u32[]{:S(2)}) collective-permute-start(f32[2,64,256]{2,1,0:T(8,128)} %slice.18), channel_id=1, source_target_pairs={{0,2},{2,4},{4,6},{6,8},{8,10},{10,12},{12,14},{14,0},{1,3},{3,5},... | collective-permute-start | bytes 393224 | tf_op jit(solution)/shard_map/ppermute | solution.py:180
  184.8 1.0 copy-start.1
  185.8 5.3 %copy-start.3 = (f32[2,128,256]{2,1,0:T(8,128)S(1)}, f32[2,128,256]{2,1,0:T(8,128)}, u32[]{:S(2)}) copy-start(f32[2,128,256]{2,1,0:T(8,128)} %copy-done.2) | copy-start | bytes 786436
  185.8 5.3 %copy-start.5 = (f32[2,128,256]{2,1,0:T(8,128)S(1)}, f32[2,128,256]{2,1,0:T(8,128)}, u32[]{:S(2)}) copy-start(f32[2,128,256]{2,1,0:T(8,128)} %copy-done.4) | copy-start | bytes 786436
